TPU v7x, 32 devices: a whole 2x2x4 slice. The times are simulated.
32 devices in a mesh: dom: 8 (over z, core), feat: 4 (over y, x).
Axes of the slice: x: 2, y: 2, z: 4, core: 2. Of those that a mesh axis runs over, the one named last changes fastest.
Arguments:
- grad_out: bfloat16 [512, 6144], P('feat', 'dom'), may hold values from -6 to 6
- saved_agg: bfloat16 [512, 6144], P('feat', 'dom'), may hold values from -0.1875 to 0.1875
- weight: bfloat16 [512, 512], P('feat'), may hold values from -0.25 to 0.25
- tile_values: bfloat16 [768, 128, 128], P('dom'), may hold values from 0 to 0.029907227
- tile_dst: int32 [768], P('dom'), may hold values from 0 to 5
- tile_slot: int32 [768], P('dom'), may hold values from 0 to 7
- tile_count: int32 [8], P('dom'), may hold values from 12 to 96, as said below
- mirror_owner: int32 [8, 8], P('dom'), may hold values from 0 to 7, each once within a row
- mirror_local: int32 [8, 8], P('dom'), may hold values from 0 to 5
Outputs:
- grad_nodes: bfloat16 [512, 6144], P('feat', 'dom')
- grad_mirrors: bfloat16 [512, 8192], P('feat', 'dom')
- weight_grad: float32 [512, 512], P('feat')
Inputs may be any that keep to these rules, and one draw needn't show every extreme that they name: Every partition's first tile_count tiles are live, the rest are padding; some partition has all 96 live in every draw. `mirror_owner`: each partition's row names every partition once.
All inputs are finite; a program needn't handle non-finite values.
Results may differ from a plain program's by a relative error of at most 0.0049.
Values may be sent and summed in bfloat16 or wider, within the bound.
A program may use at most 64 MiB of HBM per device.

v0:
```python
import jax
import jax.numpy as jnp
from jax import lax
from jax.sharding import PartitionSpec as P


def body(
    grad_out,
    saved_agg,
    weight,
    tile_values,
    tile_dst,
    tile_slot,
    tile_count,
    mirror_owner,
    mirror_local,
):
    row_count = grad_out.shape[0]
    vertices = grad_out.shape[1]
    block_count = vertices // 128
    peer_count = mirror_owner.shape[1]
    tile_total = tile_values.shape[0]
    piece = lax.all_gather(grad_out, "feat", axis=0, tiled=True)
    back_new = jnp.dot(weight, piece, preferred_element_type=jnp.float32)
    wgrad_part = lax.dot_general(
        saved_agg, piece, (((1,), (1,)), ((), ())), preferred_element_type=jnp.float32
    )
    weight_grad = lax.psum(wgrad_part, "dom")
    spread = back_new.astype(jnp.bfloat16).reshape(row_count, block_count, 128)
    dst_pick = (tile_dst[:, None] == jnp.arange(block_count, dtype=jnp.int32)[None, :]).astype(
        jnp.bfloat16
    )
    sources = jnp.einsum(
        "fbk,tb->tfk", spread, dst_pick, preferred_element_type=jnp.float32
    ).astype(jnp.bfloat16)
    products = jnp.einsum("tfk,tkj->tfj", sources, tile_values, preferred_element_type=jnp.float32)
    live_tiles = (jnp.arange(tile_total, dtype=jnp.int32) < tile_count[0]).astype(jnp.float32)
    slot_hot = (tile_slot[:, None] == jnp.arange(peer_count, dtype=jnp.int32)[None, :]).astype(
        jnp.float32
    )
    slot_hot = slot_hot * live_tiles[:, None]
    partial_value = jnp.einsum("tfj,ts->fsj", products, slot_hot, precision=lax.Precision.HIGHEST)
    owner_row = mirror_owner[0]
    local_row = mirror_local[0]
    target = owner_row * block_count + local_row
    place_hot = (
        target[:, None] == jnp.arange(peer_count * block_count, dtype=jnp.int32)[None, :]
    ).astype(jnp.float32)
    spread_all = jnp.einsum(
        "fsj,sg->fgj", partial_value, place_hot, precision=lax.Precision.HIGHEST
    )
    spread_all = spread_all.reshape(row_count, peer_count * block_count * 128)
    summed = lax.psum_scatter(spread_all, "dom", scatter_dimension=1, tiled=True)
    grad_nodes = summed.astype(jnp.bfloat16)
    all_nodes = lax.all_gather(grad_nodes, "dom", axis=1, tiled=True).reshape(
        row_count, peer_count * block_count, 128
    )
    mirrors = jnp.einsum(
        "fgj,sg->fsj", all_nodes, place_hot.astype(jnp.bfloat16), preferred_element_type=jnp.float32
    ).astype(jnp.bfloat16)
    grad_mirrors = mirrors.reshape(row_count, peer_count * 128)
    return (grad_nodes, grad_mirrors, weight_grad)


def solution(mesh):
    in_specs = (
        P("feat", "dom"),
        P("feat", "dom"),
        P("feat", None),
        P("dom", None, None),
        P("dom"),
        P("dom"),
        P("dom"),
        P("dom", None),
        P("dom", None),
    )
    out_specs = (P("feat", "dom"), P("feat", "dom"), P("feat", None))
    return jax.shard_map(body, mesh=mesh, in_specs=in_specs, out_specs=out_specs, check_vma=False)
```

profile of v0, /device:TPU:0, one launch (start us, length us, event | category | flops | bytes accessed | tf_op | source)
XLA Modules:
  0.0 173.6 jit_solution(4218476773913573307)
XLA Ops:
  7.2 0.0 copy-start
  7.2 0.0 reduce-scatter.2.cloned.1.call-start
  8.0 13.9 %all_gather.6 = bf16[512,768]{1,0:T(8,128)(2,1)S(1)} all-gather(bf16[128,768]{1,0:T(8,128)(2,1)} %param.9), channel_id=1, replica_groups=mesh['dom'=8,'feat'=4] {'feat'}, dimensions={0}, use_global_device_ids=true | all-gather | bytes 983040 | tf_op jit(solution)/shard_map/all_gather | solution.py:23
  22.0 0.0 copy-start.1
  22.0 0.9 copy-done.1
  22.9 1.2 convolution_convert_fusion.1
  24.0 0.8 copy.12
  24.9 1.1 copy.13
  26.0 0.7 add_bitcast_fusion
  26.7 1.7 fusion.9
  28.3 0.0 copy-done
  28.3 0.0 copy-start.3
  28.3 1.9 %fusion.2 = f32[96,128,128]{2,1,0:T(8,128)S(1)} fusion(bf16[96,128,128]{2,1,0:T(8,128)(2,1)S(1)} %copy-done, bf16[96,128,128]{2,0,1:T(8,128)(2,1)S(1)} %fusion.9), kind=kOutput, calls=%fused_computation.3 | convolution fusion | flops 402653184 | bytes 12582912 | tf_op jit(solution)/shard_map/tfk,tkj->tfj/dot_general | solution.py:36
  30.3 0.0 copy-done.3
  30.3 6.5 %fusion.3 = f32[128,8,128]{2,1,0:T(8,128)S(1)} fusion(f32[96,128,128]{2,1,0:T(8,128)S(1)} %fusion.2, f32[96]{0:T(128)S(1)} %compare_convert_fusion, s32[96]{0:T(128)S(1)} %copy-done.3), kind=kOutput, calls=%fused_computation.5 | convolution fusion | flops 150996480 | bytes 6816512 | tf_op jit(solution)/shard_map/tfj,ts->fsj/dot_general | solution.py:42
  36.8 1.5 fusion.16
  38.3 2.6 %copy.27 = f32[16,8,48,128]{3,1,2,0:T(8,128)} copy(f32[16,8,48,128]{3,2,1,0:T(8,128)S(1)} %bitcast.40) | data formatting | bytes 6291456
  41.0 0.0 copy-start.2
  41.0 0.0 reduce-scatter.2.cloned.1.call-update
  41.0 0.0 all-gather.2.cloned.1.call-start
  41.0 40.7 %reduce-scatter.2.cloned.1.call-done = f32[128,768]{1,0:T(8,128)} async-done(((f32[128,6144]{1,0:T(8,128)}), f32[128,768]{1,0:T(8,128)}) %reduce-scatter.2.cloned.1.call-update) | async-done | bytes 393232 | tf_op jit(solution)/shard_map/reduce_scatter | solution.py:53
  81.8 1.7 convert_element_type.33
  83.5 0.0 all-gather.2.cloned.1.call-update
  83.5 0.0 all-reduce.2.cloned.1.call-start
  83.5 0.0 copy-done.2
  83.6 2.2 %fusion.23 = f32[128,512]{1,0:T(8,128)} fusion(bf16[128,768]{1,0:T(8,128)(2,1)S(1)} %copy-done.2, bf16[512,768]{1,0:T(8,128)(2,1)} %copy-done.1), kind=kOutput, calls=%fused_computation.29 | convolution fusion | flops 100663296 | bytes 1245184 | tf_op jit(solution)/shard_map/dot_general | solution.py:25
  85.8 0.0 all-reduce.2.cloned.1.call-update
  85.8 22.2 %all-gather.2.cloned.1.call-done = bf16[128,6144]{1,0:T(8,128)(2,1)} async-done(((bf16[128,768]{1,0:T(8,128)(2,1)}), bf16[128,6144]{1,0:T(8,128)(2,1)}) %all-gather.2.cloned.1.call-update) | async-done | bytes 1572880 | tf_op jit(solution)/shard_map/all_gather | solution.py:55
  108.0 1.7 %copy.17 = bf16[16,8,48,128]{3,2,1,0:T(8,128)(2,1)S(1)} copy(bf16[16,8,48,128]{3,1,2,0:T(8,128)(2,1)} %bitcast.42) | data formatting | bytes 3145728
  109.8 0.4 convolution_convert_fusion
  110.1 0.8 copy.28
  110.9 54.5 %all-reduce.2.cloned.1.call-done = f32[128,512]{1,0:T(8,128)} async-done(((f32[128,512]{1,0:T(8,128)}), f32[128,512]{1,0:T(8,128)}) %all-reduce.2.cloned.1.call-update) | async-done | bytes 262160 | tf_op jit(solution)/shard_map/psum | solution.py:28
  165.4 1.7 copy.31
  (1 shorter events, 0.0 us)
Async XLA Ops:
  7.2 21.2 %copy-start = (bf16[96,128,128]{2,1,0:T(8,128)(2,1)S(1)}, bf16[96,128,128]{2,1,0:T(8,128)(2,1)}, u32[]{:S(2)}) copy-start(bf16[96,128,128]{2,1,0:T(8,128)(2,1)} %param.12) | copy-start | bytes 9437188
  7.2 74.6 %reduce-scatter.2.cloned.1.call-start = ((), (), s32[]{:S(2)}) async-start(), calls=%async_computation.1 | async-start | bytes 3538944 | tf_op jit(solution)/shard_map/reduce_scatter | solution.py:53
  22.0 0.9 copy-start.1
  28.3 2.0 %copy-start.3 = (s32[96]{0:T(128)S(1)}, s32[96]{0:T(128)}, u32[]{:S(2)}) copy-start(s32[96]{0:T(128)} %param.14) | copy-start | bytes 1156
  41.0 42.6 %copy-start.2 = (bf16[128,768]{1,0:T(8,128)(2,1)S(1)}, bf16[128,768]{1,0:T(8,128)(2,1)}, u32[]{:S(2)}) copy-start(bf16[128,768]{1,0:T(8,128)(2,1)} %param.10) | copy-start | bytes 589828
  41.0 67.0 %all-gather.2.cloned.1.call-start = ((), (), s32[]{:S(2)}) async-start(), calls=%async_computation.2 | async-start | bytes 1769472 | tf_op jit(solution)/shard_map/all_gather | solution.py:55
  83.5 81.9 %all-reduce.2.cloned.1.call-start = ((), (), s32[]{:S(2)}) async-start(), calls=%async_computation.3 | async-start | bytes 524288 | tf_op jit(solution)/shard_map/psum | solution.py:28
Sparse Core Ops, SparseCore 0:
  41.1 40.6 reduce-scatter.1
  84.0 24.0 all-gather.1
  110.9 54.4 all-reduce.1
where the time goes:
time: 174 us
  waiting for transfers between devices  117 us (67%)
  matrix products  15.4 us (9%)
  between operations  14.6 us (8%)
  blocking collectives  13.9 us (8%)
  local copies, waits for them, and re-layouts  9.64 us (6%)
  other arithmetic  2.37 us (1%)
    psum x1, waiting for transfers between devices, body(): weight_grad = lax.psum(wgrad_part, 'dom')  54.5 us
    reduce_scatter x1, waiting for transfers between devices, body(): lax.psum_scatter(spread_all, 'dom', scatter_dimension=1, tiled=True)  40.7 us
    all_gather x1, waiting for transfers between devices, body(): lax.all_gather(grad_nodes, 'dom', axis=1, tiled=True)  22.2 us
    all_gather x1, blocking collectives, body(): piece = lax.all_gather(grad_out, 'feat', axis=0, tiled=True)  13.9 us
    unnamed x12, local copies, waits for them, and re-layouts  7.72 us
    dot_general x1, matrix products, body(): jnp.einsum('tfj,ts->fsj', products, slot_hot, precision=lax.Precision.HIG...  6.53 us
  transfers between devices with their start and end apart: 3, of which 3 were waited for; matrix products, arithmetic and copies ran while one was open for 3% of the time, Pallas kernels for 0%

commit v1 on v0

v1 whole, which is shorter than its diff:
```python
import functools

import jax
import jax.numpy as jnp
from jax import lax
from jax.experimental import pallas as pl
from jax.experimental.pallas import tpu as pltpu
from jax.sharding import PartitionSpec as P

MESH = pl.DeviceIdType.MESH
B = 128
F32 = jnp.float32
BF16 = jnp.bfloat16


def kernel(
    n, m, vb, scatter, links, owner, local, g, s, w, tiles,
    gn_out, gm_out, wg_out,
    tbuf, run, adj, allg, spread, meta, mrec, pbuf, prec, msend, gmrec, wpart, wrec, wsum,
    tsem, g_s, g_r, m_s, m_r, p_s, p_r, b_s, b_r, ws_s, ws_r, wg_s, wg_r,
):
    me = lax.axis_index("dom")
    mf = lax.axis_index("feat")
    rows = g.shape[0]
    tile_total = tiles.shape[0]
    chunk = tile_total // 4
    dom_peers = [lax.rem(me + k, n) for k in range(1, n)]
    feat_peers = [lax.rem(mf + k, m) for k in range(1, m)]

    def load_tiles(i):
        return pltpu.make_async_copy(
            tiles.at[pl.ds(i * chunk, chunk)], tbuf.at[pl.ds(i * chunk, chunk)], tsem.at[i]
        )

    for i in range(4):
        load_tiles(i).start()

    barrier = pltpu.get_barrier_semaphore()
    for q in dom_peers:
        pl.semaphore_signal(barrier, inc=1, device_id={"dom": q}, device_id_type=MESH)
    for q in feat_peers:
        pl.semaphore_signal(barrier, inc=1, device_id={"feat": q}, device_id_type=MESH)
    pl.semaphore_wait(barrier, n + m - 2)

    def g_send(q):
        return pltpu.make_async_remote_copy(
            g, allg.at[pl.ds(pl.multiple_of(mf * rows, rows), rows)],
            g_s.at[q], g_r.at[mf], device_id={"feat": q}, device_id_type=MESH,
        )

    def g_recv(q):
        return pltpu.make_async_remote_copy(
            g, allg.at[pl.ds(pl.multiple_of(q * rows, rows), rows)],
            g_s.at[q], g_r.at[q], device_id={"feat": q}, device_id_type=MESH,
        )

    def dom_send(src, dst, send, recv, q):
        return pltpu.make_async_remote_copy(
            src, dst, send.at[q], recv.at[me], device_id={"dom": q}, device_id_type=MESH
        )

    def dom_recv(src, dst, send, recv, q):
        return pltpu.make_async_remote_copy(
            src, dst, send.at[q], recv.at[q], device_id={"dom": q}, device_id_type=MESH
        )

    for q in feat_peers:
        g_send(q).start()
    allg[pl.ds(pl.multiple_of(mf * rows, rows), rows), :] = g[...]

    def slot_of(o):
        return lax.fori_loop(
            0, n, lambda k, acc: jnp.where(owner[0, k] == o, k, acc), jnp.int32(0)
        )

    def fill_meta(o, _):
        value = local[0, slot_of(o)].astype(F32)
        meta[o] = jnp.full((16, B), value, F32).astype(BF16)
        return 0

    lax.fori_loop(0, n, fill_meta, 0)
    for q in dom_peers:
        dom_send(meta.at[q], mrec.at[me], m_s, m_r, q).start()
    mrec[me] = meta[me]

    run[0] = jnp.zeros((B, B), F32)

    def add_tile(t, _):
        run[t + 1] = run[links[t]] + tbuf[t].astype(F32)
        return 0

    for i in range(4):
        load_tiles(i).wait()
        lax.fori_loop(i * chunk, (i + 1) * chunk, add_tile, 0)

    def fill_owner(o, _):
        slot = slot_of(o)
        for d in range(vb):
            adj[d * B : (d + 1) * B, pl.ds(pl.multiple_of(o * B, B), B)] = run[
                links[tile_total + d * n + slot]
            ].astype(BF16)
        return 0

    lax.fori_loop(0, n, fill_owner, 0)

    for q in feat_peers:
        g_recv(q).wait_recv()
    spread[...] = jnp.dot(w[...], allg[...], preferred_element_type=F32).astype(BF16)

    half = n // 2
    mate = me + 1 - 2 * lax.rem(me, 2)
    for i in range(half):
        c = lax.rem(me // 2 + 1 + i, half)
        columns = pl.ds(pl.multiple_of(c * 2 * B, 2 * B), 2 * B)
        part = jnp.dot(spread[...], adj[:, columns], preferred_element_type=F32).astype(BF16)
        pbuf[2 * c] = part[:, :B]
        pbuf[2 * c + 1] = part[:, B:]
        targets = (2 * c, 2 * c + 1) if i < half - 1 else (mate,)
        for q in targets:
            dom_send(pbuf.at[q], prec.at[me], p_s, p_r, q).start()
    prec[me] = pbuf[me]

    wgrad = lax.dot_general(
        s[...], allg[...], (((1,), (1,)), ((), ())), preferred_element_type=F32
    )
    if scatter:
        wrows = rows // n

        def mine(ref, q):
            return ref.at[pl.ds(pl.multiple_of(q * wrows, wrows), wrows)]

        wpart[...] = wgrad.astype(BF16)
        for q in dom_peers:
            dom_send(mine(wpart, q), wrec.at[me], ws_s, ws_r, q).start()
        wrec[me] = wpart[pl.ds(pl.multiple_of(me * wrows, wrows), wrows), :]
    else:
        wg_out[...] = wgrad

    for q in dom_peers:
        dom_recv(meta.at[q], mrec.at[q], m_s, m_r, q).wait_recv()
    for q in dom_peers:
        dom_recv(pbuf.at[q], prec.at[q], p_s, p_r, q).wait_recv()

    rc = 32

    def sum_rows(r, _):
        here = pl.ds(pl.multiple_of(r * rc, rc), rc)
        pick = [mrec[p, 0:1, :].astype(F32) for p in range(n)]
        terms = [prec[p, here, :].astype(F32) for p in range(n)]
        back = [jnp.zeros((rc, B), F32) for _ in range(n)]
        for b in range(vb):
            hot = [jnp.where(pick[p] == b, 1.0, 0.0) for p in range(n)]
            total = terms[0] * hot[0]
            for p in range(1, n):
                total = total + terms[p] * hot[p]
            node = total.astype(BF16)
            gn_out[here, b * B : (b + 1) * B] = node
            node = node.astype(F32)
            back = [back[p] + node * hot[p] for p in range(n)]
        for p in range(n):
            msend[p, here, :] = back[p].astype(BF16)
        return 0

    lax.fori_loop(0, rows // rc, sum_rows, 0)
    for q in dom_peers:
        dom_send(msend.at[q], gmrec.at[me], b_s, b_r, q).start()
    gmrec[me] = msend[me]

    if scatter:
        for q in dom_peers:
            dom_recv(mine(wpart, q), wrec.at[q], ws_s, ws_r, q).wait_recv()
        total = wrec[0].astype(F32)
        for p in range(1, n):
            total = total + wrec[p].astype(F32)
        wsum[...] = total.astype(BF16)
        for q in dom_peers:
            dom_send(wsum, mine(wg_out, me), wg_s, wg_r, q).start()
        wg_out[pl.ds(pl.multiple_of(me * wrows, wrows), wrows), :] = wsum[...]

    for q in dom_peers:
        dom_recv(msend.at[q], gmrec.at[q], b_s, b_r, q).wait_recv()

    def place(slot, _):
        gm_out[:, pl.ds(pl.multiple_of(slot * B, B), B)] = gmrec[owner[0, slot]]
        return 0

    lax.fori_loop(0, n, place, 0)

    if scatter:
        for q in dom_peers:
            dom_recv(wsum, mine(wg_out, q), wg_s, wg_r, q).wait_recv()
    for q in feat_peers:
        g_send(q).wait_send()
    for q in dom_peers:
        dom_send(meta.at[q], mrec.at[me], m_s, m_r, q).wait_send()
        dom_send(pbuf.at[q], prec.at[me], p_s, p_r, q).wait_send()
        dom_send(msend.at[q], gmrec.at[me], b_s, b_r, q).wait_send()
        if scatter:
            dom_send(mine(wpart, q), wrec.at[me], ws_s, ws_r, q).wait_send()
            dom_send(wsum, mine(wg_out, me), wg_s, wg_r, q).wait_send()


def body(
    n, m,
    grad_out, saved_agg, weight, tile_values, tile_dst, tile_slot, tile_count,
    mirror_owner, mirror_local,
):
    rows, vertices = grad_out.shape
    features = weight.shape[1]
    vb = vertices // B
    tile_total = tile_values.shape[0]
    scatter = rows % (16 * n) == 0
    wrows = max(rows // n, 16)

    order = jnp.arange(tile_total, dtype=jnp.int32)
    key = tile_dst * n + tile_slot
    live_key = jnp.where(order < tile_count[0], key, -1)
    query = jnp.concatenate([key, jnp.arange(vb * n, dtype=jnp.int32)])
    limit = jnp.concatenate([order, jnp.full((vb * n,), tile_total, jnp.int32)])
    match = (query[:, None] == live_key[None, :]) & (order[None, :] < limit[:, None])
    links = jnp.max(jnp.where(match, order[None, :] + 1, 0), axis=1)

    vmem = pl.BlockSpec(memory_space=pltpu.VMEM)
    smem = pl.BlockSpec(memory_space=pltpu.SMEM)
    dma = pltpu.SemaphoreType.DMA
    wg_type = BF16 if scatter else F32
    gn, gm, wg = pl.pallas_call(
        functools.partial(kernel, n, m, vb, scatter),
        out_shape=(
            jax.ShapeDtypeStruct((rows, vertices), BF16),
            jax.ShapeDtypeStruct((rows, n * B), BF16),
            jax.ShapeDtypeStruct((rows, features), wg_type),
        ),
        in_specs=[smem] * 3 + [vmem] * 3 + [pl.BlockSpec(memory_space=pl.ANY)],
        out_specs=(vmem, vmem, vmem),
        scratch_shapes=[
            pltpu.VMEM((tile_total, B, B), BF16),
            pltpu.VMEM((tile_total + 1, B, B), F32),
            pltpu.VMEM((vertices, n * B), BF16),
            pltpu.VMEM((features, vertices), BF16),
            pltpu.VMEM((rows, vertices), BF16),
            pltpu.VMEM((n, 16, B), BF16),
            pltpu.VMEM((n, 16, B), BF16),
            pltpu.VMEM((n, rows, B), BF16),
            pltpu.VMEM((n, rows, B), BF16),
            pltpu.VMEM((n, rows, B), BF16),
            pltpu.VMEM((n, rows, B), BF16),
            pltpu.VMEM((rows, features), BF16),
            pltpu.VMEM((n, wrows, features), BF16),
            pltpu.VMEM((wrows, features), BF16),
            dma((4,)),
            dma((m,)), dma((m,)),
            dma((n,)), dma((n,)),
            dma((n,)), dma((n,)),
            dma((n,)), dma((n,)),
            dma((n,)), dma((n,)),
            dma((n,)), dma((n,)),
        ],
        compiler_params=pltpu.CompilerParams(
            collective_id=0, has_side_effects=True, vmem_limit_bytes=48 * 1024 * 1024
        ),
        cost_estimate=pl.CostEstimate(
            flops=2 * rows * vertices * (2 * features + n * B),
            bytes_accessed=2 * tile_total * B * B + 8 * rows * vertices,
            transcendentals=0,
        ),
    )(links, mirror_owner, mirror_local, grad_out, saved_agg, weight, tile_values)
    if scatter:
        wg = wg.astype(F32)
    else:
        wg = lax.psum(wg, "dom")
    return gn, gm, wg


def solution(mesh):
    in_specs = (
        P("feat", "dom"),
        P("feat", "dom"),
        P("feat", None),
        P("dom", None, None),
        P("dom"),
        P("dom"),
        P("dom"),
        P("dom", None),
        P("dom", None),
    )
    out_specs = (P("feat", "dom"), P("feat", "dom"), P("feat", None))
    return jax.shard_map(
        functools.partial(body, mesh.shape["dom"], mesh.shape["feat"]),
        mesh=mesh, in_specs=in_specs, out_specs=out_specs, check_vma=False,
    )
```

time: 174 us -> 47 us (0.27)
  waiting for transfers between devices: 117 us -> 0 us
  Pallas kernels: 0 us -> 35.7 us
  matrix products: 15.4 us -> 0 us
  blocking collectives: 13.9 us -> 0 us
  between operations: 14.6 us -> 1.31 us
  local copies, waits for them, and re-layouts: 9.64 us -> 7.33 us
    psum x1 -> x0, waiting for transfers between devices: 54.5 us -> none  [body(): weight_grad = lax.psum(wgrad_part, 'dom')]
    reduce_scatter x1 -> x0, waiting for transfers between devices: 40.7 us -> none  [body(): lax.psum_scatter(spread_all, 'dom', scatter_dimension=1, tiled=True)]
    pallas_call x0 -> x1, Pallas kernels: none -> 35.7 us  [body(): pl.pallas_call(functools.partial(kernel, n, m, vb, scatter), out_shape=(j...]
    all_gather x1 -> x0, waiting for transfers between devices: 22.2 us -> none  [body(): lax.all_gather(grad_nodes, 'dom', axis=1, tiled=True)]
    dot_general x7 -> x0, matrix products: 15.4 us -> none  [the longest x1 6.53 us: body(): jnp.einsum('tfj,ts->fsj', products, slot_hot, precision=lax.Precision.HIG...]
    all_gather x1 -> x0, blocking collectives: 13.9 us -> none  [body(): piece = lax.all_gather(grad_out, 'feat', axis=0, tiled=True)]
    unnamed x12 -> x14, local copies, waits for them, and re-layouts: 7.72 us -> 7.33 us
  transfers between devices with their start and end apart: 3 -> 0, of which waited for: 3 -> 0; matrix products, arithmetic and copies ran while one was open for 3% -> 0% of each run, Pallas kernels for 0% -> 0%
where the time goes in v1:
time: 47 us; the launch traced here: 46.7 us
  Pallas kernels  35.7 us (76%)
  local copies, waits for them, and re-layouts  7.33 us (16%)
  other arithmetic  2.35 us (5%)
  between operations  1.31 us (3%)
    pallas_call x1, Pallas kernels, body(): pl.pallas_call(functools.partial(kernel, n, m, vb, scatter), out_shape=(j...  35.7 us
    unnamed x14, local copies, waits for them, and re-layouts  7.33 us

profile of v1, /device:TPU:0, one launch (start us, length us, event | category | flops | bytes accessed | tf_op | source)
XLA Modules:
  0.0 46.7 jit_solution(18245674782467755586)
XLA Ops:
  1.3 0.7 %compare_select_fusion = (s32[96]{0:T(128)S(1)}, s32[96]{0:T(128)S(1)}, s32[96]{0:T(128)S(1)}) fusion(s32[]{:T(128)} %bitcast.1, s32[96]{0:T(128)} %param.14, s32[96]{0:T(128)} %param.13), kind=kLoop, calls=%fused_computation.3 | loop fusion | flops 480 | bytes 1924 | tf_op jit(solution)/shard_map/jit(_where)/select_n | solution.py:217
  2.0 0.1 pad_add_fusion
  2.0 0.9 %select_reduce_fusion.links = s32[144]{0:T(256)S(1)} fusion(s32[96]{0:T(128)S(1)} %get-tuple-element.11, s32[144]{0:T(256)} %constant.3.clone.1, s32[96]{0:T(128)S(1)} %get-tuple-element.9, s32[144]{0:T(256)S(1)} %pad_add_fusion), kind=kLoop, calls=%fused_computation | loop fusion | flops 68976 | bytes 2496 | tf_op jit(solution)/shard_map/reduce_max | solution.py:221
  2.9 0.0 copy-start
  2.9 1.9 %copy-done = bf16[96,128,128]{2,1,0:T(8,128)(2,1)S(1)} copy-done((bf16[96,128,128]{2,1,0:T(8,128)(2,1)S(1)}, bf16[96,128,128]{2,1,0:T(8,128)(2,1)}, u32[]{:S(2)}) %copy-start) | copy-done | bytes 3145752
  4.8 0.0 copy-start.1
  4.8 0.9 %copy-done.1 = bf16[128,768]{1,0:T(8,128)(2,1)S(1)} copy-done((bf16[128,768]{1,0:T(8,128)(2,1)S(1)}, bf16[128,768]{1,0:T(8,128)(2,1)}, u32[]{:S(2)}) %copy-start.1) | copy-done | bytes 196632
  5.7 0.0 copy-start.2
  5.7 0.9 %copy-done.2 = bf16[128,768]{1,0:T(8,128)(2,1)S(1)} copy-done((bf16[128,768]{1,0:T(8,128)(2,1)S(1)}, bf16[128,768]{1,0:T(8,128)(2,1)}, u32[]{:S(2)}) %copy-start.2) | copy-done | bytes 196632
  6.7 0.0 copy-start.3
  6.7 0.9 %copy-done.3 = bf16[128,512]{1,0:T(8,128)(2,1)S(1)} copy-done((bf16[128,512]{1,0:T(8,128)(2,1)S(1)}, bf16[128,512]{1,0:T(8,128)(2,1)}, u32[]{:S(2)}) %copy-start.3) | copy-done | bytes 131096
  7.6 0.0 copy-start.4
  7.6 0.7 %copy-done.4 = s32[1,8]{1,0:T(1,128)S(1)} copy-done((s32[1,8]{1,0:T(1,128)S(1)}, s32[1,8]{1,0:T(1,128)}, u32[]{:S(2)}) %copy-start.4) | copy-done | bytes 56
  8.2 0.0 copy-start.5
  8.2 0.7 %copy-done.5 = s32[1,8]{1,0:T(1,128)S(1)} copy-done((s32[1,8]{1,0:T(1,128)S(1)}, s32[1,8]{1,0:T(1,128)}, u32[]{:S(2)}) %copy-start.5) | copy-done | bytes 56
  8.9 35.7 %shard_map.112 = (bf16[128,768]{1,0:T(8,128)(2,1)S(1)}, bf16[128,1024]{1,0:T(8,128)(2,1)S(1)}, bf16[128,512]{1,0:T(8,128)(2,1)S(1)}) custom-call(s32[144]{0:T(256)S(1)} %select_reduce_fusion.links, s32[1,8]{1,0:T(1,128)S(1)} %copy-done.4, s32[1,8]{1,0:T(1,128)S(1)} %copy-done.5, bf16[128,768]{1,0:T(8,128)(2,1)S(1)} %copy-done.1, ...), custom_call_target="tpu_custom_call" | custom-call | flops 402653184 | bytes 3932160 | tf_op jit(solution)/shard_map/pallas_call | solution.py:227
  44.6 0.7 %convert_element_type.3 = f32[128,512]{1,0:T(8,128)} convert(bf16[128,512]{1,0:T(8,128)(2,1)S(1)} %get-tuple-element.8) | non-fusion elementwise | flops 65536 | bytes 393216 | tf_op jit(solution)/shard_map/convert_element_type | solution.py:269
  45.3 0.7 %copy.15 = bf16[128,768]{1,0:T(8,128)(2,1)} copy(bf16[128,768]{1,0:T(8,128)(2,1)S(1)} %get-tuple-element.15) | data formatting | bytes 393216
  46.0 0.7 %copy.16 = bf16[128,1024]{1,0:T(8,128)(2,1)} copy(bf16[128,1024]{1,0:T(8,128)(2,1)S(1)} %get-tuple-element.16) | data formatting | bytes 524288
  (1 shorter events, 0.0 us)
Async XLA Ops:
  2.9 1.9 %copy-start = (bf16[96,128,128]{2,1,0:T(8,128)(2,1)S(1)}, bf16[96,128,128]{2,1,0:T(8,128)(2,1)}, u32[]{:S(2)}) copy-start(bf16[96,128,128]{2,1,0:T(8,128)(2,1)} %tiles.1) | copy-start | bytes 9437188
  4.8 0.9 %copy-start.1 = (bf16[128,768]{1,0:T(8,128)(2,1)S(1)}, bf16[128,768]{1,0:T(8,128)(2,1)}, u32[]{:S(2)}) copy-start(bf16[128,768]{1,0:T(8,128)(2,1)} %g.1) | copy-start | bytes 589828
  5.7 0.9 %copy-start.2 = (bf16[128,768]{1,0:T(8,128)(2,1)S(1)}, bf16[128,768]{1,0:T(8,128)(2,1)}, u32[]{:S(2)}) copy-start(bf16[128,768]{1,0:T(8,128)(2,1)} %s.1) | copy-start | bytes 589828
  6.7 0.9 %copy-start.3 = (bf16[128,512]{1,0:T(8,128)(2,1)S(1)}, bf16[128,512]{1,0:T(8,128)(2,1)}, u32[]{:S(2)}) copy-start(bf16[128,512]{1,0:T(8,128)(2,1)} %w.1) | copy-start | bytes 393220
  7.6 0.7 %copy-start.4 = (s32[1,8]{1,0:T(1,128)S(1)}, s32[1,8]{1,0:T(1,128)}, u32[]{:S(2)}) copy-start(s32[1,8]{1,0:T(1,128)} %owner.1) | copy-start | bytes 100
  8.2 0.7 %copy-start.5 = (s32[1,8]{1,0:T(1,128)S(1)}, s32[1,8]{1,0:T(1,128)}, u32[]{:S(2)}) copy-start(s32[1,8]{1,0:T(1,128)} %local.1) | copy-start | bytes 100

commit v2 on v1

--- a/solution.py
+++ b/solution.py
@@ -14,24 +14,40 @@
 
 
 def kernel(
-    n, m, vb, scatter, links, owner, local, g, s, w, tiles,
+    n, m, vb, scatter, dst_hbm, slot_hbm, count_hbm, owner_hbm, local_hbm, g, s_hbm, w_hbm, tiles,
     gn_out, gm_out, wg_out,
-    tbuf, run, adj, allg, spread, meta, mrec, pbuf, prec, msend, gmrec, wpart, wrec, wsum,
-    tsem, g_s, g_r, m_s, m_r, p_s, p_r, b_s, b_r, ws_s, ws_r, wg_s, wg_r,
+    dst, slots, count, owner, local, s, w, tbuf, tile_link_v, pair_link_v, tile_link, pair_link,
+    slot_of, run, adj, allg, spread, meta, mrec, pbuf, prec, msend, gmrec, gn, gm, wg,
+    wpart, wmate, wsend, wrec, wsum,
+    lsem, tsem, g_s, g_r, m_s, m_r, p_s, p_r, b_s, b_r, ws_s, ws_r, wg_s, wg_r, x_sem,
 ):
     me = lax.axis_index("dom")
     mf = lax.axis_index("feat")
     rows = g.shape[0]
     tile_total = tiles.shape[0]
+    pairs = vb * n
     chunk = tile_total // 4
     dom_peers = [lax.rem(me + k, n) for k in range(1, n)]
     feat_peers = [lax.rem(mf + k, m) for k in range(1, m)]
+    core = lax.rem(me, 2)
+    mate = me + 1 - 2 * core
+    line_peers = [lax.rem(me + 2 * k, n) for k in range(1, n // 2)]
 
     def load_tiles(i):
         return pltpu.make_async_copy(
             tiles.at[pl.ds(i * chunk, chunk)], tbuf.at[pl.ds(i * chunk, chunk)], tsem.at[i]
         )
 
+    my_rows = pl.ds(pl.multiple_of(mf * rows, rows), rows)
+    loads = [
+        pltpu.make_async_copy(a, b, lsem.at[i])
+        for i, (a, b) in enumerate(
+            [(dst_hbm, dst), (slot_hbm, slots), (count_hbm, count), (owner_hbm, owner),
+             (local_hbm, local), (w_hbm, w), (s_hbm, s), (g, allg.at[my_rows])]
+        )
+    ]
+    for load in loads:
+        load.start()
     for i in range(4):
         load_tiles(i).start()
 
@@ -66,15 +82,34 @@
 
     for q in feat_peers:
         g_send(q).start()
-    allg[pl.ds(pl.multiple_of(mf * rows, rows), rows), :] = g[...]
-
-    def slot_of(o):
-        return lax.fori_loop(
-            0, n, lambda k, acc: jnp.where(owner[0, k] == o, k, acc), jnp.int32(0)
-        )
+    for load in loads[:5]:
+        load.wait()
+
+    key = dst[...] * n + slots[...]
+    across = lax.broadcasted_iota(jnp.int32, (tile_total, tile_total), 1)
+    down = lax.broadcasted_iota(jnp.int32, (tile_total, tile_total), 0)
+    key_row = jnp.broadcast_to(key, (tile_total, tile_total))
+    key_column = jnp.sum(jnp.where(across == down, key_row, 0), axis=1, keepdims=True)
+    live_tiles = count[0, 0]
+    same = (key_column == key_row) & (down < live_tiles) & (down < across)
+    tile_link_v[...] = jnp.max(jnp.where(same, down + 1, 0), axis=0, keepdims=True)
+    pair = lax.broadcasted_iota(jnp.int32, (tile_total, pairs), 1)
+    down = lax.broadcasted_iota(jnp.int32, (tile_total, pairs), 0)
+    same = (key_column == pair) & (down < live_tiles)
+    pair_link_v[...] = jnp.max(jnp.where(same, down + 1, 0), axis=0, keepdims=True)
+    link_copies = [
+        pltpu.make_async_copy(tile_link_v, tile_link, lsem.at[8]),
+        pltpu.make_async_copy(pair_link_v, pair_link, lsem.at[9]),
+    ]
+    for copy in link_copies:
+        copy.start()
 
     def fill_meta(o, _):
-        value = local[0, slot_of(o)].astype(F32)
+        slot = lax.fori_loop(
+            0, n, lambda k, acc: jnp.where(owner[0, k] == o, k, acc), jnp.int32(0), unroll=8
+        )
+        slot_of[o] = slot
+        value = local[0, slot].astype(F32)
         meta[o] = jnp.full((16, B), value, F32).astype(BF16)
         return 0
 
@@ -83,32 +118,35 @@
         dom_send(meta.at[q], mrec.at[me], m_s, m_r, q).start()
     mrec[me] = meta[me]
 
+    for copy in link_copies:
+        copy.wait()
     run[0] = jnp.zeros((B, B), F32)
 
     def add_tile(t, _):
-        run[t + 1] = run[links[t]] + tbuf[t].astype(F32)
+        run[t + 1] = run[tile_link[0, t]] + tbuf[t].astype(F32)
         return 0
 
     for i in range(4):
         load_tiles(i).wait()
-        lax.fori_loop(i * chunk, (i + 1) * chunk, add_tile, 0)
+        lax.fori_loop(i * chunk, (i + 1) * chunk, add_tile, 0, unroll=4)
 
     def fill_owner(o, _):
-        slot = slot_of(o)
+        slot = slot_of[o]
         for d in range(vb):
             adj[d * B : (d + 1) * B, pl.ds(pl.multiple_of(o * B, B), B)] = run[
-                links[tile_total + d * n + slot]
+                pair_link[0, d * n + slot]
             ].astype(BF16)
         return 0
 
     lax.fori_loop(0, n, fill_owner, 0)
 
+    for load in loads[5:]:
+        load.wait()
     for q in feat_peers:
         g_recv(q).wait_recv()
     spread[...] = jnp.dot(w[...], allg[...], preferred_element_type=F32).astype(BF16)
 
     half = n // 2
-    mate = me + 1 - 2 * lax.rem(me, 2)
     for i in range(half):
         c = lax.rem(me // 2 + 1 + i, half)
         columns = pl.ds(pl.multiple_of(c * 2 * B, 2 * B), 2 * B)
@@ -125,16 +163,29 @@
     )
     if scatter:
         wrows = rows // n
-
-        def mine(ref, q):
-            return ref.at[pl.ds(pl.multiple_of(q * wrows, wrows), wrows)]
-
         wpart[...] = wgrad.astype(BF16)
-        for q in dom_peers:
-            dom_send(mine(wpart, q), wrec.at[me], ws_s, ws_r, q).start()
-        wrec[me] = wpart[pl.ds(pl.multiple_of(me * wrows, wrows), wrows), :]
+
+        def span(ref, start, size):
+            return ref.at[pl.ds(pl.multiple_of(start, wrows), size)]
+
+        def piece(q):
+            return (lax.rem(q, 2) * half + q // 2) * wrows
+
+        swap = pltpu.make_async_remote_copy(
+            span(wpart, (1 - core) * half * wrows, half * wrows), wmate,
+            x_sem.at[0], x_sem.at[1], device_id={"dom": mate}, device_id_type=MESH,
+        )
+        swap.start()
+        swap.wait()
+        mine = wpart[pl.ds(pl.multiple_of(core * half * wrows, wrows), half * wrows), :]
+        wsend[...] = (mine.astype(F32) + wmate[...].astype(F32)).astype(BF16)
+        for q in line_peers:
+            dom_send(span(wsend, q // 2 * wrows, wrows), wrec.at[me // 2], ws_s, ws_r, q).start()
+        wrec[me // 2] = wsend[pl.ds(pl.multiple_of(me // 2 * wrows, wrows), wrows), :]
     else:
-        wg_out[...] = wgrad
+        wg[...] = wgrad
+        flush_wg = pltpu.make_async_copy(wg, wg_out, lsem.at[10])
+        flush_wg.start()
 
     for q in dom_peers:
         dom_recv(meta.at[q], mrec.at[q], m_s, m_r, q).wait_recv()
@@ -154,7 +205,7 @@
             for p in range(1, n):
                 total = total + terms[p] * hot[p]
             node = total.astype(BF16)
-            gn_out[here, b * B : (b + 1) * B] = node
+            gn[here, b * B : (b + 1) * B] = node
             node = node.astype(F32)
             back = [back[p] + node * hot[p] for p in range(n)]
         for p in range(n):
@@ -164,40 +215,75 @@
     lax.fori_loop(0, rows // rc, sum_rows, 0)
     for q in dom_peers:
         dom_send(msend.at[q], gmrec.at[me], b_s, b_r, q).start()
+    flush_gn = pltpu.make_async_copy(gn, gn_out, lsem.at[11])
+    flush_gn.start()
     gmrec[me] = msend[me]
 
     if scatter:
-        for q in dom_peers:
-            dom_recv(mine(wpart, q), wrec.at[q], ws_s, ws_r, q).wait_recv()
+        for q in line_peers:
+            dom_recv(span(wsend, q // 2 * wrows, wrows), wrec.at[q // 2], ws_s, ws_r, q).wait_recv()
         total = wrec[0].astype(F32)
-        for p in range(1, n):
+        for p in range(1, half):
             total = total + wrec[p].astype(F32)
         wsum[...] = total.astype(BF16)
-        for q in dom_peers:
-            dom_send(wsum, mine(wg_out, me), wg_s, wg_r, q).start()
-        wg_out[pl.ds(pl.multiple_of(me * wrows, wrows), wrows), :] = wsum[...]
+        for q in line_peers:
+            dom_send(wsum, span(wg, piece(me), wrows), wg_s, wg_r, q).start()
+        wg[pl.ds(pl.multiple_of(piece(me), wrows), wrows), :] = wsum[...]
+        for q in line_peers:
+            dom_recv(wsum, span(wg, piece(q), wrows), wg_s, wg_r, q).wait_recv()
+        half_rows = span(wg, core * half * wrows, half * wrows)
+        give = pltpu.make_async_remote_copy(
+            half_rows, half_rows, x_sem.at[2], x_sem.at[3],
+            device_id={"dom": mate}, device_id_type=MESH,
+        )
+        give.start()
 
     for q in dom_peers:
         dom_recv(msend.at[q], gmrec.at[q], b_s, b_r, q).wait_recv()
 
     def place(slot, _):
-        gm_out[:, pl.ds(pl.multiple_of(slot * B, B), B)] = gmrec[owner[0, slot]]
+        gm[:, pl.ds(pl.multiple_of(slot * B, B), B)] = gmrec[owner[0, slot]]
         return 0
 
-    lax.fori_loop(0, n, place, 0)
+    lax.fori_loop(0, n, place, 0, unroll=4)
+    flush_gm = pltpu.make_async_copy(gm, gm_out, lsem.at[12])
+    flush_gm.start()
 
     if scatter:
-        for q in dom_peers:
-            dom_recv(wsum, mine(wg_out, q), wg_s, wg_r, q).wait_recv()
+        give.wait()
+        flush_wg = pltpu.make_async_copy(wg, wg_out, lsem.at[10])
+        flush_wg.start()
     for q in feat_peers:
         g_send(q).wait_send()
     for q in dom_peers:
         dom_send(meta.at[q], mrec.at[me], m_s, m_r, q).wait_send()
         dom_send(pbuf.at[q], prec.at[me], p_s, p_r, q).wait_send()
         dom_send(msend.at[q], gmrec.at[me], b_s, b_r, q).wait_send()
-        if scatter:
-            dom_send(mine(wpart, q), wrec.at[me], ws_s, ws_r, q).wait_send()
-            dom_send(wsum, mine(wg_out, me), wg_s, wg_r, q).wait_send()
+    if scatter:
+        for q in line_peers:
+            dom_send(span(wsend, q // 2 * wrows, wrows), wrec.at[me // 2], ws_s, ws_r, q).wait_send()
+            dom_send(wsum, span(wg, piece(me), wrows), wg_s, wg_r, q).wait_send()
+    flush_gn.wait()
+    flush_gm.wait()
+    flush_wg.wait()
+
+
+def finish(gn, gm, wg, gn_out, gm_out, wg_out, narrow, wide, sem):
+    copies = [
+        pltpu.make_async_copy(gn, gn_out, sem.at[0]),
+        pltpu.make_async_copy(gm, gm_out, sem.at[1]),
+    ]
+    load = pltpu.make_async_copy(wg, narrow, sem.at[2])
+    load.start()
+    for copy in copies:
+        copy.start()
+    load.wait()
+    wide[...] = narrow[...].astype(F32)
+    store = pltpu.make_async_copy(wide, wg_out, sem.at[3])
+    store.start()
+    for copy in copies:
+        copy.wait()
+    store.wait()
 
 
 def body(
@@ -212,16 +298,10 @@
     scatter = rows % (16 * n) == 0
     wrows = max(rows // n, 16)
 
-    order = jnp.arange(tile_total, dtype=jnp.int32)
-    key = tile_dst * n + tile_slot
-    live_key = jnp.where(order < tile_count[0], key, -1)
-    query = jnp.concatenate([key, jnp.arange(vb * n, dtype=jnp.int32)])
-    limit = jnp.concatenate([order, jnp.full((vb * n,), tile_total, jnp.int32)])
-    match = (query[:, None] == live_key[None, :]) & (order[None, :] < limit[:, None])
-    links = jnp.max(jnp.where(match, order[None, :] + 1, 0), axis=1)
-
-    vmem = pl.BlockSpec(memory_space=pltpu.VMEM)
-    smem = pl.BlockSpec(memory_space=pltpu.SMEM)
+    hbm = pl.BlockSpec(memory_space=pltpu.HBM)
+    int_rows = functools.partial(pltpu.VMEM, dtype=jnp.int32)
+    int_smem = functools.partial(pltpu.SMEM, dtype=jnp.int32)
+    pairs = vb * n
     dma = pltpu.SemaphoreType.DMA
     wg_type = BF16 if scatter else F32
     gn, gm, wg = pl.pallas_call(
@@ -231,10 +311,22 @@
             jax.ShapeDtypeStruct((rows, n * B), BF16),
             jax.ShapeDtypeStruct((rows, features), wg_type),
         ),
-        in_specs=[smem] * 3 + [vmem] * 3 + [pl.BlockSpec(memory_space=pl.ANY)],
-        out_specs=(vmem, vmem, vmem),
+        in_specs=[hbm] * 9,
+        out_specs=(hbm, hbm, hbm),
         scratch_shapes=[
+            int_rows((1, tile_total)),
+            int_rows((1, tile_total)),
+            int_smem((1, 1)),
+            int_smem((1, n)),
+            int_smem((1, n)),
+            pltpu.VMEM((rows, vertices), BF16),
+            pltpu.VMEM((rows, features), BF16),
             pltpu.VMEM((tile_total, B, B), BF16),
+            int_rows((1, tile_total)),
+            int_rows((1, pairs)),
+            int_smem((1, tile_total)),
+            int_smem((1, pairs)),
+            int_smem((n,)),
             pltpu.VMEM((tile_total + 1, B, B), F32),
             pltpu.VMEM((vertices, n * B), BF16),
             pltpu.VMEM((features, vertices), BF16),
@@ -245,9 +337,15 @@
             pltpu.VMEM((n, rows, B), BF16),
             pltpu.VMEM((n, rows, B), BF16),
             pltpu.VMEM((n, rows, B), BF16),
+            pltpu.VMEM((rows, vertices), BF16),
+            pltpu.VMEM((rows, n * B), BF16),
+            pltpu.VMEM((rows, features), wg_type),
             pltpu.VMEM((rows, features), BF16),
-            pltpu.VMEM((n, wrows, features), BF16),
+            pltpu.VMEM((wrows * n // 2, features), BF16),
+            pltpu.VMEM((wrows * n // 2, features), BF16),
+            pltpu.VMEM((n // 2, wrows, features), BF16),
             pltpu.VMEM((wrows, features), BF16),
+            dma((13,)),
             dma((4,)),
             dma((m,)), dma((m,)),
             dma((n,)), dma((n,)),
@@ -255,18 +353,34 @@
             dma((n,)), dma((n,)),
             dma((n,)), dma((n,)),
             dma((n,)), dma((n,)),
+            dma((4,)),
         ],
         compiler_params=pltpu.CompilerParams(
-            collective_id=0, has_side_effects=True, vmem_limit_bytes=48 * 1024 * 1024
+            collective_id=0, has_side_effects=True, vmem_limit_bytes=62 * 1024 * 1024
         ),
         cost_estimate=pl.CostEstimate(
             flops=2 * rows * vertices * (2 * features + n * B),
             bytes_accessed=2 * tile_total * B * B + 8 * rows * vertices,
             transcendentals=0,
         ),
-    )(links, mirror_owner, mirror_local, grad_out, saved_agg, weight, tile_values)
+    )(
+        tile_dst.reshape(1, -1), tile_slot.reshape(1, -1), tile_count.reshape(1, 1),
+        mirror_owner, mirror_local, grad_out, saved_agg, weight, tile_values,
+    )
     if scatter:
-        wg = wg.astype(F32)
+        return pl.pallas_call(
+            finish,
+            out_shape=(
+                jax.ShapeDtypeStruct(gn.shape, BF16),
+                jax.ShapeDtypeStruct(gm.shape, BF16),
+                jax.ShapeDtypeStruct(wg.shape, F32),
+            ),
+            in_specs=[hbm] * 3,
+            out_specs=(hbm, hbm, hbm),
+            scratch_shapes=[
+                pltpu.VMEM(wg.shape, BF16), pltpu.VMEM(wg.shape, F32), dma((4,))
+            ],
+        )(gn, gm, wg)
     else:
         wg = lax.psum(wg, "dom")
     return gn, gm, wg

time: 47 us -> 52 us (1.11)
  Pallas kernels: 35.7 us -> 50.6 us
  local copies, waits for them, and re-layouts: 7.33 us -> 0 us
  other arithmetic: 2.35 us -> 0 us
    pallas_call x0 -> x1, Pallas kernels: none -> 15 us  [body(): pl.pallas_call(finish, out_shape=(jax.ShapeDtypeStruct(gn.shape, BF16), j...]
    unnamed x14 -> x0, local copies, waits for them, and re-layouts: 7.33 us -> none
    reduce_max x1 -> x0, other arithmetic: 0.86 us -> none  [body(): links = jnp.max(jnp.where(match, order[None, :] + 1, 0), axis=1)]
    convert_element_type x1 -> x0, other arithmetic: 0.73 us -> none  [body(): wg = wg.astype(F32)]
    select_n x1 -> x0, other arithmetic: 0.68 us -> none  [body(): live_key = jnp.where(order < tile_count[0], key, -1)]
where the time goes in v2:
time: 52 us; the launch traced here: 51.9 us
  Pallas kernels  50.6 us (97%)
  between operations  1.29 us (2%)
    pallas_call x1, Pallas kernels, body(): pl.pallas_call(functools.partial(kernel, n, m, vb, scatter), out_shape=(j...  35.6 us
    pallas_call x1, Pallas kernels, body(): pl.pallas_call(finish, out_shape=(jax.ShapeDtypeStruct(gn.shape, BF16), j...  15 us

profile of v2, /device:TPU:0, one launch (start us, length us, event | category | flops | bytes accessed | tf_op | source)
XLA Modules:
  0.0 51.9 jit_solution(6899588339380260544)
XLA Ops:
  1.3 35.6 %shard_map.112 = (bf16[128,768]{1,0:T(8,128)(2,1)}, bf16[128,1024]{1,0:T(8,128)(2,1)}, bf16[128,512]{1,0:T(8,128)(2,1)}) custom-call(s32[1,96]{1,0:T(1,128)} %bitcast.4, s32[1,96]{1,0:T(1,128)} %bitcast.5, s32[1,1]{1,0:T(1,128)} %bitcast.3.count_hbm, s32[1,8]{1,0:T(1,128)} %owner_hbm.1, s32[1,8]{1,0:T(1,128)} %local_hbm.1, bf16[128,768]{1,0:T(8,128)(2,1)} %g.1, ...), custom_call_target="tpu_custom_call" | custom-call | flops 402653184 | bytes 3932160 | tf_op jit(solution)/shard_map/pallas_call | solution.py:307
  36.8 15.0 %shard_map.113 = (bf16[128,768]{1,0:T(8,128)(2,1)}, bf16[128,1024]{1,0:T(8,128)(2,1)}, f32[128,512]{1,0:T(8,128)}) custom-call(bf16[128,768]{1,0:T(8,128)(2,1)} %get-tuple-element.6.gn, bf16[128,1024]{1,0:T(8,128)(2,1)} %get-tuple-element.7.gm, bf16[128,512]{1,0:T(8,128)(2,1)} %get-tuple-element.8.wg), custom_call_target="tpu_custom_call" | custom-call | tf_op jit(solution)/shard_map/pallas_call | solution.py:371

commit v3 on v2

--- a/solution.py
+++ b/solution.py
@@ -17,7 +17,7 @@
     n, m, vb, scatter, dst_hbm, slot_hbm, count_hbm, owner_hbm, local_hbm, g, s_hbm, w_hbm, tiles,
     gn_out, gm_out, wg_out,
     dst, slots, count, owner, local, s, w, tbuf, tile_link_v, pair_link_v, tile_link, pair_link,
-    slot_of, run, adj, allg, spread, meta, mrec, pbuf, prec, msend, gmrec, gn, gm, wg,
+    slot_of, run, adj, allg, spread, meta, mrec, pbuf, prec, msend, gmrec0, gmrec1, gn, gm, wg,
     wpart, wmate, wsend, wrec, wsum,
     lsem, tsem, g_s, g_r, m_s, m_r, p_s, p_r, b_s, b_r, ws_s, ws_r, wg_s, wg_r, x_sem,
 ):
@@ -58,17 +58,38 @@
         pl.semaphore_signal(barrier, inc=1, device_id={"feat": q}, device_id_type=MESH)
     pl.semaphore_wait(barrier, n + m - 2)
 
-    def g_send(q):
+    half_rows = rows // 2
+    square = m == 4
+    near = mf + 1 - 2 * lax.rem(mf, 2)
+    far = lax.rem(mf + 2, 4)
+    across_both = lax.rem(near + 2, 4)
+
+    def g_copy(source, part, sem, to, whole=False):
+        size = rows if whole else half_rows
+        start = source * rows + part * half_rows
+        there = allg.at[pl.ds(pl.multiple_of(start, half_rows), size)]
+        here = there
+        if source is mf:
+            here = g.at[pl.ds(part * half_rows, size)]
         return pltpu.make_async_remote_copy(
-            g, allg.at[pl.ds(pl.multiple_of(mf * rows, rows), rows)],
-            g_s.at[q], g_r.at[mf], device_id={"feat": q}, device_id_type=MESH,
-        )
-
-    def g_recv(q):
-        return pltpu.make_async_remote_copy(
-            g, allg.at[pl.ds(pl.multiple_of(q * rows, rows), rows)],
-            g_s.at[q], g_r.at[q], device_id={"feat": q}, device_id_type=MESH,
-        )
+            here, there, g_s.at[sem], g_r.at[sem], device_id={"feat": to}, device_id_type=MESH
+        )
+
+    if square:
+        own_sends = [
+            g_copy(mf, 0, 0, near), g_copy(mf, 1, 2, far),
+            g_copy(mf, 1, 1, near), g_copy(mf, 0, 3, far),
+        ]
+        passed = [g_copy(near, 0, 4, far), g_copy(far, 1, 5, near)]
+        first = [g_copy(near, 0, 0, near), g_copy(far, 1, 2, far)]
+        second = [g_copy(near, 1, 1, near), g_copy(far, 0, 3, far)]
+        last = [g_copy(across_both, 0, 4, far), g_copy(across_both, 1, 5, near)]
+    else:
+        own_sends = [g_copy(mf, 0, k, q, True) for k, q in enumerate(feat_peers)]
+        passed, first, second = [], [], []
+        last = [
+            g_copy(lax.rem(mf + m - 1 - k, m), 0, k, mf, True) for k in range(m - 1)
+        ]
 
     def dom_send(src, dst, send, recv, q):
         return pltpu.make_async_remote_copy(
@@ -80,8 +101,8 @@
             src, dst, send.at[q], recv.at[q], device_id={"dom": q}, device_id_type=MESH
         )
 
-    for q in feat_peers:
-        g_send(q).start()
+    for copy in own_sends:
+        copy.start()
     for load in loads[:5]:
         load.wait()
 
@@ -129,6 +150,10 @@
     for i in range(4):
         load_tiles(i).wait()
         lax.fori_loop(i * chunk, (i + 1) * chunk, add_tile, 0, unroll=4)
+        if i == 1:
+            for arrived, on in zip(first, passed):
+                arrived.wait_recv()
+                on.start()
 
     def fill_owner(o, _):
         slot = slot_of[o]
@@ -142,21 +167,43 @@
 
     for load in loads[5:]:
         load.wait()
-    for q in feat_peers:
-        g_recv(q).wait_recv()
+    for copy in second + last:
+        copy.wait_recv()
     spread[...] = jnp.dot(w[...], allg[...], preferred_element_type=F32).astype(BF16)
 
     half = n // 2
+    def p_copy(h, q, sending):
+        recv = p_r.at[h * n + (me if sending else q)]
+        return pltpu.make_async_remote_copy(
+            pbuf.at[h, q], prec.at[h, me if sending else q], p_s.at[h * n + q], recv,
+            device_id={"dom": q}, device_id_type=MESH,
+        )
+
+    gmrec = (gmrec0, gmrec1)
+
+    def b_copy(h, q, sending):
+        recv = b_r.at[h * n + (me if sending else q)]
+        return pltpu.make_async_remote_copy(
+            msend.at[h, q], gmrec[h].at[me if sending else q], b_s.at[h * n + q], recv,
+            device_id={"dom": q}, device_id_type=MESH,
+        )
+
+    order = []
     for i in range(half):
         c = lax.rem(me // 2 + 1 + i, half)
         columns = pl.ds(pl.multiple_of(c * 2 * B, 2 * B), 2 * B)
         part = jnp.dot(spread[...], adj[:, columns], preferred_element_type=F32).astype(BF16)
-        pbuf[2 * c] = part[:, :B]
-        pbuf[2 * c + 1] = part[:, B:]
+        for h in range(2):
+            pbuf[h, 2 * c] = part[h * half_rows : (h + 1) * half_rows, :B]
+            pbuf[h, 2 * c + 1] = part[h * half_rows : (h + 1) * half_rows, B:]
         targets = (2 * c, 2 * c + 1) if i < half - 1 else (mate,)
         for q in targets:
-            dom_send(pbuf.at[q], prec.at[me], p_s, p_r, q).start()
-    prec[me] = pbuf[me]
+            p_copy(0, q, True).start()
+            order.append(q)
+    for q in order:
+        p_copy(1, q, True).start()
+    for h in range(2):
+        prec[h, me] = pbuf[h, me]
 
     wgrad = lax.dot_general(
         s[...], allg[...], (((1,), (1,)), ((), ())), preferred_element_type=F32
@@ -176,12 +223,6 @@
             x_sem.at[0], x_sem.at[1], device_id={"dom": mate}, device_id_type=MESH,
         )
         swap.start()
-        swap.wait()
-        mine = wpart[pl.ds(pl.multiple_of(core * half * wrows, wrows), half * wrows), :]
-        wsend[...] = (mine.astype(F32) + wmate[...].astype(F32)).astype(BF16)
-        for q in line_peers:
-            dom_send(span(wsend, q // 2 * wrows, wrows), wrec.at[me // 2], ws_s, ws_r, q).start()
-        wrec[me // 2] = wsend[pl.ds(pl.multiple_of(me // 2 * wrows, wrows), wrows), :]
     else:
         wg[...] = wgrad
         flush_wg = pltpu.make_async_copy(wg, wg_out, lsem.at[10])
@@ -189,15 +230,13 @@
 
     for q in dom_peers:
         dom_recv(meta.at[q], mrec.at[q], m_s, m_r, q).wait_recv()
-    for q in dom_peers:
-        dom_recv(pbuf.at[q], prec.at[q], p_s, p_r, q).wait_recv()
-
-    rc = 32
-
-    def sum_rows(r, _):
+    rc = min(32, half_rows)
+
+    def sum_rows(h, r, _):
         here = pl.ds(pl.multiple_of(r * rc, rc), rc)
+        there = pl.ds(pl.multiple_of(h * half_rows + r * rc, rc), rc)
         pick = [mrec[p, 0:1, :].astype(F32) for p in range(n)]
-        terms = [prec[p, here, :].astype(F32) for p in range(n)]
+        terms = [prec[h, p, here, :].astype(F32) for p in range(n)]
         back = [jnp.zeros((rc, B), F32) for _ in range(n)]
         for b in range(vb):
             hot = [jnp.where(pick[p] == b, 1.0, 0.0) for p in range(n)]
@@ -205,20 +244,29 @@
             for p in range(1, n):
                 total = total + terms[p] * hot[p]
             node = total.astype(BF16)
-            gn[here, b * B : (b + 1) * B] = node
+            gn[there, b * B : (b + 1) * B] = node
             node = node.astype(F32)
             back = [back[p] + node * hot[p] for p in range(n)]
         for p in range(n):
-            msend[p, here, :] = back[p].astype(BF16)
+            msend[h, p, here, :] = back[p].astype(BF16)
         return 0
 
-    lax.fori_loop(0, rows // rc, sum_rows, 0)
-    for q in dom_peers:
-        dom_send(msend.at[q], gmrec.at[me], b_s, b_r, q).start()
+    for h in range(2):
+        for q in order:
+            p_copy(h, q, False).wait_recv()
+        lax.fori_loop(0, half_rows // rc, functools.partial(sum_rows, h), 0)
+        for q in order:
+            b_copy(h, q, True).start()
+        gmrec[h][me] = msend[h, me]
+        if scatter and h == 0:
+            swap.wait()
+            mine = wpart[pl.ds(pl.multiple_of(core * half * wrows, wrows), half * wrows), :]
+            wsend[...] = (mine.astype(F32) + wmate[...].astype(F32)).astype(BF16)
+            for q in line_peers:
+                dom_send(span(wsend, q // 2 * wrows, wrows), wrec.at[me // 2], ws_s, ws_r, q).start()
+            wrec[me // 2] = wsend[pl.ds(pl.multiple_of(me // 2 * wrows, wrows), wrows), :]
     flush_gn = pltpu.make_async_copy(gn, gn_out, lsem.at[11])
     flush_gn.start()
-    gmrec[me] = msend[me]
-
     if scatter:
         for q in line_peers:
             dom_recv(span(wsend, q // 2 * wrows, wrows), wrec.at[q // 2], ws_s, ws_r, q).wait_recv()
@@ -231,59 +279,63 @@
         wg[pl.ds(pl.multiple_of(piece(me), wrows), wrows), :] = wsum[...]
         for q in line_peers:
             dom_recv(wsum, span(wg, piece(q), wrows), wg_s, wg_r, q).wait_recv()
-        half_rows = span(wg, core * half * wrows, half * wrows)
+        kept = span(wg, core * half * wrows, half * wrows)
         give = pltpu.make_async_remote_copy(
-            half_rows, half_rows, x_sem.at[2], x_sem.at[3],
+            kept, kept, x_sem.at[2], x_sem.at[3],
             device_id={"dom": mate}, device_id_type=MESH,
         )
         give.start()
 
-    for q in dom_peers:
-        dom_recv(msend.at[q], gmrec.at[q], b_s, b_r, q).wait_recv()
-
-    def place(slot, _):
-        gm[:, pl.ds(pl.multiple_of(slot * B, B), B)] = gmrec[owner[0, slot]]
+    def place(h, slot, _):
+        gm[h * half_rows : (h + 1) * half_rows, pl.ds(pl.multiple_of(slot * B, B), B)] = gmrec[h][
+            owner[0, slot]
+        ]
         return 0
 
-    lax.fori_loop(0, n, place, 0, unroll=4)
-    flush_gm = pltpu.make_async_copy(gm, gm_out, lsem.at[12])
-    flush_gm.start()
+    flush_gm = []
+    for h in range(2):
+        for q in order:
+            b_copy(h, q, False).wait_recv()
+        lax.fori_loop(0, n, functools.partial(place, h), 0, unroll=4)
+        part = pl.ds(h * half_rows, half_rows)
+        flush_gm.append(pltpu.make_async_copy(gm.at[part], gm_out.at[part], lsem.at[12 + h]))
+        flush_gm[h].start()
 
     if scatter:
         give.wait()
         flush_wg = pltpu.make_async_copy(wg, wg_out, lsem.at[10])
         flush_wg.start()
-    for q in feat_peers:
-        g_send(q).wait_send()
+    for copy in own_sends + passed:
+        copy.wait_send()
     for q in dom_peers:
         dom_send(meta.at[q], mrec.at[me], m_s, m_r, q).wait_send()
-        dom_send(pbuf.at[q], prec.at[me], p_s, p_r, q).wait_send()
-        dom_send(msend.at[q], gmrec.at[me], b_s, b_r, q).wait_send()
+        for h in range(2):
+            p_copy(h, q, True).wait_send()
+            b_copy(h, q, True).wait_send()
     if scatter:
         for q in line_peers:
             dom_send(span(wsend, q // 2 * wrows, wrows), wrec.at[me // 2], ws_s, ws_r, q).wait_send()
             dom_send(wsum, span(wg, piece(me), wrows), wg_s, wg_r, q).wait_send()
     flush_gn.wait()
-    flush_gm.wait()
+    for copy in flush_gm:
+        copy.wait()
     flush_wg.wait()
 
 
-def finish(gn, gm, wg, gn_out, gm_out, wg_out, narrow, wide, sem):
-    copies = [
-        pltpu.make_async_copy(gn, gn_out, sem.at[0]),
-        pltpu.make_async_copy(gm, gm_out, sem.at[1]),
-    ]
-    load = pltpu.make_async_copy(wg, narrow, sem.at[2])
-    load.start()
-    for copy in copies:
-        copy.start()
-    load.wait()
+def finish(gn, gm, wg, gn_out, gm_out, wg_out, gn_v, gm_v, narrow, wide, sem):
+    pairs = ((wg, narrow, wide, wg_out), (gm, gm_v, gm_v, gm_out), (gn, gn_v, gn_v, gn_out))
+    loads = [pltpu.make_async_copy(p[0], p[1], sem.at[k]) for k, p in enumerate(pairs)]
+    stores = [pltpu.make_async_copy(p[2], p[3], sem.at[3 + k]) for k, p in enumerate(pairs)]
+    for load in loads:
+        load.start()
+    loads[0].wait()
     wide[...] = narrow[...].astype(F32)
-    store = pltpu.make_async_copy(wide, wg_out, sem.at[3])
-    store.start()
-    for copy in copies:
-        copy.wait()
-    store.wait()
+    stores[0].start()
+    for k in (1, 2):
+        loads[k].wait()
+        stores[k].start()
+    for store in stores:
+        store.wait()
 
 
 def body(
@@ -333,10 +385,11 @@
             pltpu.VMEM((rows, vertices), BF16),
             pltpu.VMEM((n, 16, B), BF16),
             pltpu.VMEM((n, 16, B), BF16),
-            pltpu.VMEM((n, rows, B), BF16),
-            pltpu.VMEM((n, rows, B), BF16),
-            pltpu.VMEM((n, rows, B), BF16),
-            pltpu.VMEM((n, rows, B), BF16),
+            pltpu.VMEM((2, n, rows // 2, B), BF16),
+            pltpu.VMEM((2, n, rows // 2, B), BF16),
+            pltpu.VMEM((2, n, rows // 2, B), BF16),
+            pltpu.VMEM((n, rows // 2, B), BF16),
+            pltpu.VMEM((n, rows // 2, B), BF16),
             pltpu.VMEM((rows, vertices), BF16),
             pltpu.VMEM((rows, n * B), BF16),
             pltpu.VMEM((rows, features), wg_type),
@@ -345,12 +398,12 @@
             pltpu.VMEM((wrows * n // 2, features), BF16),
             pltpu.VMEM((n // 2, wrows, features), BF16),
             pltpu.VMEM((wrows, features), BF16),
-            dma((13,)),
+            dma((14,)),
             dma((4,)),
-            dma((m,)), dma((m,)),
+            dma((max(m, 6),)), dma((max(m, 6),)),
             dma((n,)), dma((n,)),
-            dma((n,)), dma((n,)),
-            dma((n,)), dma((n,)),
+            dma((2 * n,)), dma((2 * n,)),
+            dma((2 * n,)), dma((2 * n,)),
             dma((n,)), dma((n,)),
             dma((n,)), dma((n,)),
             dma((4,)),
@@ -378,7 +431,8 @@
             in_specs=[hbm] * 3,
             out_specs=(hbm, hbm, hbm),
             scratch_shapes=[
-                pltpu.VMEM(wg.shape, BF16), pltpu.VMEM(wg.shape, F32), dma((4,))
+                pltpu.VMEM(gn.shape, BF16), pltpu.VMEM(gm.shape, BF16),
+                pltpu.VMEM(wg.shape, BF16), pltpu.VMEM(wg.shape, F32), dma((6,)),
             ],
         )(gn, gm, wg)
     else:

time: 52 us -> 37.7 us (0.73)
  Pallas kernels: 50.6 us -> 36.2 us
    pallas_call x1, Pallas kernels: 15 us -> 1.84 us  [body(): pl.pallas_call(finish, out_shape=(jax.ShapeDtypeStruct(gn.shape, BF16), j...]
    pallas_call x1, Pallas kernels: 35.6 us -> 34.4 us  [body(): pl.pallas_call(functools.partial(kernel, n, m, vb, scatter), out_shape=(j...]
where the time goes in v3:
time: 37.7 us; the launch traced here: 37.5 us
  Pallas kernels  36.2 us (96%)
  between operations  1.29 us (3%)
    pallas_call x1, Pallas kernels, body(): pl.pallas_call(functools.partial(kernel, n, m, vb, scatter), out_shape=(j...  34.4 us
    pallas_call x1, Pallas kernels, body(): pl.pallas_call(finish, out_shape=(jax.ShapeDtypeStruct(gn.shape, BF16), j...  1.84 us

profile of v3, /device:TPU:0, one launch (start us, length us, event | category | flops | bytes accessed | tf_op | source)
XLA Modules:
  0.0 37.5 jit_solution(126896184056548902)
XLA Ops:
  1.3 34.4 %shard_map.112 = (bf16[128,768]{1,0:T(8,128)(2,1)}, bf16[128,1024]{1,0:T(8,128)(2,1)}, bf16[128,512]{1,0:T(8,128)(2,1)}) custom-call(s32[1,96]{1,0:T(1,128)} %bitcast.4, s32[1,96]{1,0:T(1,128)} %bitcast.5, s32[1,1]{1,0:T(1,128)} %bitcast.3.count_hbm, s32[1,8]{1,0:T(1,128)} %owner_hbm.1, s32[1,8]{1,0:T(1,128)} %local_hbm.1, bf16[128,768]{1,0:T(8,128)(2,1)} %g.1, ...), custom_call_target="tpu_custom_call" | custom-call | flops 402653184 | bytes 3932160 | tf_op jit(solution)/shard_map/pallas_call | solution.py:359
  35.7 1.8 %shard_map.113 = (bf16[128,768]{1,0:T(8,128)(2,1)}, bf16[128,1024]{1,0:T(8,128)(2,1)}, f32[128,512]{1,0:T(8,128)}) custom-call(bf16[128,768]{1,0:T(8,128)(2,1)} %get-tuple-element.6.gn, bf16[128,1024]{1,0:T(8,128)(2,1)} %get-tuple-element.7.gm, bf16[128,512]{1,0:T(8,128)(2,1)} %get-tuple-element.8.wg), custom_call_target="tpu_custom_call" | custom-call | tf_op jit(solution)/shard_map/pallas_call | solution.py:424

commit v4 on v3

--- a/solution.py
+++ b/solution.py
@@ -16,7 +16,8 @@
 def kernel(
     n, m, vb, scatter, dst_hbm, slot_hbm, count_hbm, owner_hbm, local_hbm, g, s_hbm, w_hbm, tiles,
     gn_out, gm_out, wg_out,
-    dst, slots, count, owner, local, s, w, tbuf, tile_link_v, pair_link_v, tile_link, pair_link,
+    dst, slots, count, owner, local, s, w, tbuf, tile_order_v, joins_v, pair_end_v, tile_order,
+    joins, pair_end,
     slot_of, run, adj, allg, spread, meta, mrec, pbuf, prec, msend, gmrec0, gmrec1, gn, gm, wg,
     wpart, wmate, wsend, wrec, wsum,
     lsem, tsem, g_s, g_r, m_s, m_r, p_s, p_r, b_s, b_r, ws_s, ws_r, wg_s, wg_r, x_sem,
@@ -106,21 +107,27 @@
     for load in loads[:5]:
         load.wait()
 
-    key = dst[...] * n + slots[...]
     across = lax.broadcasted_iota(jnp.int32, (tile_total, tile_total), 1)
     down = lax.broadcasted_iota(jnp.int32, (tile_total, tile_total), 0)
-    key_row = jnp.broadcast_to(key, (tile_total, tile_total))
+    key = jnp.broadcast_to(dst[...] * n + slots[...], (tile_total, tile_total))
+    key_row = jnp.where(across < count[0, 0], key, pairs)
     key_column = jnp.sum(jnp.where(across == down, key_row, 0), axis=1, keepdims=True)
-    live_tiles = count[0, 0]
-    same = (key_column == key_row) & (down < live_tiles) & (down < across)
-    tile_link_v[...] = jnp.max(jnp.where(same, down + 1, 0), axis=0, keepdims=True)
+    earlier = (key_row == key_column) & (across < down)
+    rank = jnp.sum(
+        jnp.where((key_row < key_column) | earlier, 1, 0), axis=1, keepdims=True
+    )
+    joined = jnp.max(jnp.where(earlier, 1, 0), axis=1, keepdims=True)
+    here = rank == across
+    tile_order_v[...] = jnp.sum(jnp.where(here, down, 0), axis=0, keepdims=True)
+    joins_v[...] = jnp.sum(jnp.where(here, joined, 0), axis=0, keepdims=True)
     pair = lax.broadcasted_iota(jnp.int32, (tile_total, pairs), 1)
-    down = lax.broadcasted_iota(jnp.int32, (tile_total, pairs), 0)
-    same = (key_column == pair) & (down < live_tiles)
-    pair_link_v[...] = jnp.max(jnp.where(same, down + 1, 0), axis=0, keepdims=True)
+    upto = jnp.sum(jnp.where(key_column <= pair, 1, 0), axis=0, keepdims=True)
+    found = jnp.max(jnp.where(key_column == pair, 1, 0), axis=0, keepdims=True)
+    pair_end_v[...] = upto * found
     link_copies = [
-        pltpu.make_async_copy(tile_link_v, tile_link, lsem.at[8]),
-        pltpu.make_async_copy(pair_link_v, pair_link, lsem.at[9]),
+        pltpu.make_async_copy(tile_order_v, tile_order, lsem.at[8]),
+        pltpu.make_async_copy(joins_v, joins, lsem.at[14]),
+        pltpu.make_async_copy(pair_end_v, pair_end, lsem.at[9]),
     ]
     for copy in link_copies:
         copy.start()
@@ -141,15 +148,18 @@
 
     for copy in link_copies:
         copy.wait()
-    run[0] = jnp.zeros((B, B), F32)
-
-    def add_tile(t, _):
-        run[t + 1] = run[tile_link[0, t]] + tbuf[t].astype(F32)
-        return 0
-
+    run[0] = jnp.zeros((B, B), BF16)
     for i in range(4):
         load_tiles(i).wait()
-        lax.fori_loop(i * chunk, (i + 1) * chunk, add_tile, 0, unroll=4)
+
+    def add_tile(t, acc):
+        acc = acc * joins[0, t].astype(F32) + tbuf[tile_order[0, t]].astype(F32)
+        run[t + 1] = acc.astype(BF16)
+        return acc
+
+    acc = jnp.zeros((B, B), F32)
+    for i in range(4):
+        acc = lax.fori_loop(i * chunk, (i + 1) * chunk, add_tile, acc, unroll=4)
         if i == 1:
             for arrived, on in zip(first, passed):
                 arrived.wait_recv()
@@ -159,8 +169,8 @@
         slot = slot_of[o]
         for d in range(vb):
             adj[d * B : (d + 1) * B, pl.ds(pl.multiple_of(o * B, B), B)] = run[
-                pair_link[0, d * n + slot]
-            ].astype(BF16)
+                pair_end[0, d * n + slot]
+            ]
         return 0
 
     lax.fori_loop(0, n, fill_owner, 0)
@@ -375,11 +385,13 @@
             pltpu.VMEM((rows, features), BF16),
             pltpu.VMEM((tile_total, B, B), BF16),
             int_rows((1, tile_total)),
+            int_rows((1, tile_total)),
             int_rows((1, pairs)),
+            int_smem((1, tile_total)),
             int_smem((1, tile_total)),
             int_smem((1, pairs)),
             int_smem((n,)),
-            pltpu.VMEM((tile_total + 1, B, B), F32),
+            pltpu.VMEM((tile_total + 1, B, B), BF16),
             pltpu.VMEM((vertices, n * B), BF16),
             pltpu.VMEM((features, vertices), BF16),
             pltpu.VMEM((rows, vertices), BF16),
@@ -398,7 +410,7 @@
             pltpu.VMEM((wrows * n // 2, features), BF16),
             pltpu.VMEM((n // 2, wrows, features), BF16),
             pltpu.VMEM((wrows, features), BF16),
-            dma((14,)),
+            dma((15,)),
             dma((4,)),
             dma((max(m, 6),)), dma((max(m, 6),)),
             dma((n,)), dma((n,)),

time: 37.7 us -> 37.7 us (level)
  no operation moved by 1% of the time
where the time goes in v4:
time: 37.7 us; the launch traced here: 37.5 us
  Pallas kernels  36.2 us (96%)
  between operations  1.29 us (3%)
    pallas_call x1, Pallas kernels, body(): pl.pallas_call(functools.partial(kernel, n, m, vb, scatter), out_shape=(j...  34.4 us
    pallas_call x1, Pallas kernels, body(): pl.pallas_call(finish, out_shape=(jax.ShapeDtypeStruct(gn.shape, BF16), j...  1.84 us

profile of v4, /device:TPU:0, one launch (start us, length us, event | category | flops | bytes accessed | tf_op | source)
XLA Modules:
  0.0 37.5 jit_solution(12596943919755739860)
XLA Ops:
  1.3 34.4 %shard_map.112 = (bf16[128,768]{1,0:T(8,128)(2,1)}, bf16[128,1024]{1,0:T(8,128)(2,1)}, bf16[128,512]{1,0:T(8,128)(2,1)}) custom-call(s32[1,96]{1,0:T(1,128)} %bitcast.4, s32[1,96]{1,0:T(1,128)} %bitcast.5, s32[1,1]{1,0:T(1,128)} %bitcast.3.count_hbm, s32[1,8]{1,0:T(1,128)} %owner_hbm.1, s32[1,8]{1,0:T(1,128)} %local_hbm.1, bf16[128,768]{1,0:T(8,128)(2,1)} %g.1, ...), custom_call_target="tpu_custom_call" | custom-call | flops 402653184 | bytes 3932160 | tf_op jit(solution)/shard_map/pallas_call | solution.py:369
  35.7 1.8 %shard_map.113 = (bf16[128,768]{1,0:T(8,128)(2,1)}, bf16[128,1024]{1,0:T(8,128)(2,1)}, f32[128,512]{1,0:T(8,128)}) custom-call(bf16[128,768]{1,0:T(8,128)(2,1)} %get-tuple-element.6.gn, bf16[128,1024]{1,0:T(8,128)(2,1)} %get-tuple-element.7.gm, bf16[128,512]{1,0:T(8,128)(2,1)} %get-tuple-element.8.wg), custom_call_target="tpu_custom_call" | custom-call | tf_op jit(solution)/shard_map/pallas_call | solution.py:436

commit v5 on v4

--- a/solution.py
+++ b/solution.py
@@ -177,9 +177,37 @@
 
     for load in loads[5:]:
         load.wait()
-    for copy in second + last:
-        copy.wait_recv()
-    spread[...] = jnp.dot(w[...], allg[...], preferred_element_type=F32).astype(BF16)
+
+    def piece_rows(source):
+        return pl.ds(pl.multiple_of(source * rows, rows), rows)
+
+    def back_part(source):
+        here = piece_rows(source)
+        return jnp.dot(w[:, here], allg[here, :], preferred_element_type=F32)
+
+    def wgrad_part(source):
+        here = piece_rows(source)
+        value = lax.dot_general(
+            s[...], allg[here, :], (((1,), (1,)), ((), ())), preferred_element_type=F32
+        )
+        wpart[:, here] = value.astype(BF16)
+
+    pieces = square and scatter and rows % B == 0
+    if pieces:
+        back = back_part(mf)
+        wgrad_part(mf)
+        for copy in second:
+            copy.wait_recv()
+        back = back + back_part(near) + back_part(far)
+        wgrad_part(near)
+        wgrad_part(far)
+        for copy in last:
+            copy.wait_recv()
+        spread[...] = (back + back_part(across_both)).astype(BF16)
+    else:
+        for copy in second + last:
+            copy.wait_recv()
+        spread[...] = jnp.dot(w[...], allg[...], preferred_element_type=F32).astype(BF16)
 
     half = n // 2
     def p_copy(h, q, sending):
@@ -215,12 +243,16 @@
     for h in range(2):
         prec[h, me] = pbuf[h, me]
 
-    wgrad = lax.dot_general(
-        s[...], allg[...], (((1,), (1,)), ((), ())), preferred_element_type=F32
-    )
+    if pieces:
+        wgrad_part(across_both)
+    else:
+        wgrad = lax.dot_general(
+            s[...], allg[...], (((1,), (1,)), ((), ())), preferred_element_type=F32
+        )
     if scatter:
         wrows = rows // n
-        wpart[...] = wgrad.astype(BF16)
+        if not pieces:
+            wpart[...] = wgrad.astype(BF16)
 
         def span(ref, start, size):
             return ref.at[pl.ds(pl.multiple_of(start, wrows), size)]

time: 37.7 us -> 37.6 us (level)
  no operation moved by 1% of the time
where the time goes in v5:
time: 37.6 us; the launch traced here: 37.5 us
  Pallas kernels  36.2 us (96%)
  between operations  1.29 us (3%)
    pallas_call x1, Pallas kernels, body(): pl.pallas_call(functools.partial(kernel, n, m, vb, scatter), out_shape=(j...  34.3 us
    pallas_call x1, Pallas kernels, body(): pl.pallas_call(finish, out_shape=(jax.ShapeDtypeStruct(gn.shape, BF16), j...  1.84 us

profile of v5, /device:TPU:0, one launch (start us, length us, event | category | flops | bytes accessed | tf_op | source)
XLA Modules:
  0.0 37.5 jit_solution(3516993736644451260)
XLA Ops:
  1.3 34.3 %shard_map.112 = (bf16[128,768]{1,0:T(8,128)(2,1)}, bf16[128,1024]{1,0:T(8,128)(2,1)}, bf16[128,512]{1,0:T(8,128)(2,1)}) custom-call(s32[1,96]{1,0:T(1,128)} %bitcast.4, s32[1,96]{1,0:T(1,128)} %bitcast.5, s32[1,1]{1,0:T(1,128)} %bitcast.3.count_hbm, s32[1,8]{1,0:T(1,128)} %owner_hbm.1, s32[1,8]{1,0:T(1,128)} %local_hbm.1, bf16[128,768]{1,0:T(8,128)(2,1)} %g.1, ...), custom_call_target="tpu_custom_call" | custom-call | flops 402653184 | bytes 3932160 | tf_op jit(solution)/shard_map/pallas_call | solution.py:401
  35.6 1.8 %shard_map.113 = (bf16[128,768]{1,0:T(8,128)(2,1)}, bf16[128,1024]{1,0:T(8,128)(2,1)}, f32[128,512]{1,0:T(8,128)}) custom-call(bf16[128,768]{1,0:T(8,128)(2,1)} %get-tuple-element.6.gn, bf16[128,1024]{1,0:T(8,128)(2,1)} %get-tuple-element.7.gm, bf16[128,512]{1,0:T(8,128)(2,1)} %get-tuple-element.8.wg), custom_call_target="tpu_custom_call" | custom-call | tf_op jit(solution)/shard_map/pallas_call | solution.py:468

commit v6 on v5

--- a/solution.py
+++ b/solution.py
@@ -238,8 +238,6 @@
         for q in targets:
             p_copy(0, q, True).start()
             order.append(q)
-    for q in order:
-        p_copy(1, q, True).start()
     for h in range(2):
         prec[h, me] = pbuf[h, me]
 
@@ -265,10 +263,19 @@
             x_sem.at[0], x_sem.at[1], device_id={"dom": mate}, device_id_type=MESH,
         )
         swap.start()
+        swap.wait()
+        mine = wpart[pl.ds(pl.multiple_of(core * half * wrows, wrows), half * wrows), :]
+        wsend[...] = (mine.astype(F32) + wmate[...].astype(F32)).astype(BF16)
+        for q in line_peers:
+            dom_send(span(wsend, q // 2 * wrows, wrows), wrec.at[me // 2], ws_s, ws_r, q).start()
+        wrec[me // 2] = wsend[pl.ds(pl.multiple_of(me // 2 * wrows, wrows), wrows), :]
     else:
         wg[...] = wgrad
         flush_wg = pltpu.make_async_copy(wg, wg_out, lsem.at[10])
         flush_wg.start()
+
+    for q in order:
+        p_copy(1, q, True).start()
 
     for q in dom_peers:
         dom_recv(meta.at[q], mrec.at[q], m_s, m_r, q).wait_recv()
@@ -301,24 +308,20 @@
             b_copy(h, q, True).start()
         gmrec[h][me] = msend[h, me]
         if scatter and h == 0:
-            swap.wait()
-            mine = wpart[pl.ds(pl.multiple_of(core * half * wrows, wrows), half * wrows), :]
-            wsend[...] = (mine.astype(F32) + wmate[...].astype(F32)).astype(BF16)
             for q in line_peers:
-                dom_send(span(wsend, q // 2 * wrows, wrows), wrec.at[me // 2], ws_s, ws_r, q).start()
-            wrec[me // 2] = wsend[pl.ds(pl.multiple_of(me // 2 * wrows, wrows), wrows), :]
+                dom_recv(
+                    span(wsend, q // 2 * wrows, wrows), wrec.at[q // 2], ws_s, ws_r, q
+                ).wait_recv()
+            total = wrec[0].astype(F32)
+            for p in range(1, half):
+                total = total + wrec[p].astype(F32)
+            wsum[...] = total.astype(BF16)
+            for q in line_peers:
+                dom_send(wsum, span(wg, piece(me), wrows), wg_s, wg_r, q).start()
+            wg[pl.ds(pl.multiple_of(piece(me), wrows), wrows), :] = wsum[...]
     flush_gn = pltpu.make_async_copy(gn, gn_out, lsem.at[11])
     flush_gn.start()
     if scatter:
-        for q in line_peers:
-            dom_recv(span(wsend, q // 2 * wrows, wrows), wrec.at[q // 2], ws_s, ws_r, q).wait_recv()
-        total = wrec[0].astype(F32)
-        for p in range(1, half):
-            total = total + wrec[p].astype(F32)
-        wsum[...] = total.astype(BF16)
-        for q in line_peers:
-            dom_send(wsum, span(wg, piece(me), wrows), wg_s, wg_r, q).start()
-        wg[pl.ds(pl.multiple_of(piece(me), wrows), wrows), :] = wsum[...]
         for q in line_peers:
             dom_recv(wsum, span(wg, piece(q), wrows), wg_s, wg_r, q).wait_recv()
         kept = span(wg, core * half * wrows, half * wrows)

time: 37.6 us -> 34.6 us (0.920)
  Pallas kernels: 36.2 us -> 33.1 us
    pallas_call x1, Pallas kernels: 34.3 us -> 31.3 us  [body(): pl.pallas_call(functools.partial(kernel, n, m, vb, scatter), out_shape=(j...]
where the time goes in v6:
time: 34.6 us; the launch traced here: 34.4 us
  Pallas kernels  33.1 us (96%)
  between operations  1.29 us (4%)
    pallas_call x1, Pallas kernels, body(): pl.pallas_call(functools.partial(kernel, n, m, vb, scatter), out_shape=(j...  31.3 us
    pallas_call x1, Pallas kernels, body(): pl.pallas_call(finish, out_shape=(jax.ShapeDtypeStruct(gn.shape, BF16), j...  1.84 us

profile of v6, /device:TPU:0, one launch (start us, length us, event | category | flops | bytes accessed | tf_op | source)
XLA Modules:
  0.0 34.4 jit_solution(8103069537132136693)
XLA Ops:
  1.3 31.3 %shard_map.112 = (bf16[128,768]{1,0:T(8,128)(2,1)}, bf16[128,1024]{1,0:T(8,128)(2,1)}, bf16[128,512]{1,0:T(8,128)(2,1)}) custom-call(s32[1,96]{1,0:T(1,128)} %bitcast.4, s32[1,96]{1,0:T(1,128)} %bitcast.5, s32[1,1]{1,0:T(1,128)} %bitcast.3.count_hbm, s32[1,8]{1,0:T(1,128)} %owner_hbm.1, s32[1,8]{1,0:T(1,128)} %local_hbm.1, bf16[128,768]{1,0:T(8,128)(2,1)} %g.1, ...), custom_call_target="tpu_custom_call" | custom-call | flops 402653184 | bytes 3932160 | tf_op jit(solution)/shard_map/pallas_call | solution.py:404
  32.6 1.8 %shard_map.113 = (bf16[128,768]{1,0:T(8,128)(2,1)}, bf16[128,1024]{1,0:T(8,128)(2,1)}, f32[128,512]{1,0:T(8,128)}) custom-call(bf16[128,768]{1,0:T(8,128)(2,1)} %get-tuple-element.6.gn, bf16[128,1024]{1,0:T(8,128)(2,1)} %get-tuple-element.7.gm, bf16[128,512]{1,0:T(8,128)(2,1)} %get-tuple-element.8.wg), custom_call_target="tpu_custom_call" | custom-call | tf_op jit(solution)/shard_map/pallas_call | solution.py:471

commit v7 on v6

--- a/solution.py
+++ b/solution.py
@@ -185,22 +185,65 @@
         here = piece_rows(source)
         return jnp.dot(w[:, here], allg[here, :], preferred_element_type=F32)
 
-    def wgrad_part(source):
+    def wgrad_part(source, k):
         here = piece_rows(source)
         value = lax.dot_general(
             s[...], allg[here, :], (((1,), (1,)), ((), ())), preferred_element_type=F32
         )
-        wpart[:, here] = value.astype(BF16)
+        wpart[:, k * B : (k + 1) * B] = value.astype(BF16)
 
     pieces = square and scatter and rows % B == 0
+    half = n // 2
+    wrows = rows // n
+    features = w.shape[1]
+    groups = ((0, features - B), (features - B, B)) if pieces else ((0, 0), (0, features))
+
+    def span(ref, start, size, g=None):
+        here = pl.ds(pl.multiple_of(start, wrows), size)
+        return ref.at[here] if g is None else ref.at[here, pl.ds(*groups[g])]
+
+    def piece(q):
+        return (lax.rem(q, 2) * half + q // 2) * wrows
+
+    def swap_copy(g):
+        return pltpu.make_async_remote_copy(
+            span(wpart, (1 - core) * half * wrows, half * wrows, g),
+            wmate.at[:, pl.ds(*groups[g])],
+            x_sem.at[4 * g], x_sem.at[4 * g + 1], device_id={"dom": mate}, device_id_type=MESH,
+        )
+
+    def line_copy(g, q, sending):
+        there = me // 2 if sending else q // 2
+        return pltpu.make_async_remote_copy(
+            span(wsend, q // 2 * wrows, wrows, g), wrec.at[there, :, pl.ds(*groups[g])],
+            ws_s.at[g * n + q], ws_r.at[g * n + (me if sending else q)],
+            device_id={"dom": q}, device_id_type=MESH,
+        )
+
+    def swap_start(g):
+        swap_copy(g).start()
+
+    def pair_sum(g):
+        swap_copy(g).wait()
+        lanes = pl.ds(*groups[g])
+        mine = wpart[pl.ds(pl.multiple_of(core * half * wrows, wrows), half * wrows), lanes]
+        wsend[:, lanes] = (mine.astype(F32) + wmate[:, lanes].astype(F32)).astype(BF16)
+        for q in line_peers:
+            line_copy(g, q, True).start()
+        own = wsend[pl.ds(pl.multiple_of(me // 2 * wrows, wrows), wrows), lanes]
+        wrec[me // 2, :, lanes] = own
+
+    used_groups = (0, 1) if pieces else (1,)
     if pieces:
         back = back_part(mf)
-        wgrad_part(mf)
+        wgrad_part(mf, 0)
         for copy in second:
             copy.wait_recv()
         back = back + back_part(near) + back_part(far)
-        wgrad_part(near)
-        wgrad_part(far)
+        wgrad_part(near, 1)
+        wgrad_part(far, 2)
+        swap_start(0)
+        pair_sum(0)
         for copy in last:
             copy.wait_recv()
         spread[...] = (back + back_part(across_both)).astype(BF16)
@@ -209,7 +252,6 @@
             copy.wait_recv()
         spread[...] = jnp.dot(w[...], allg[...], preferred_element_type=F32).astype(BF16)
 
-    half = n // 2
     def p_copy(h, q, sending):
         recv = p_r.at[h * n + (me if sending else q)]
         return pltpu.make_async_remote_copy(
@@ -242,33 +284,17 @@
         prec[h, me] = pbuf[h, me]
 
     if pieces:
-        wgrad_part(across_both)
+        wgrad_part(across_both, 3)
     else:
         wgrad = lax.dot_general(
             s[...], allg[...], (((1,), (1,)), ((), ())), preferred_element_type=F32
         )
     if scatter:
-        wrows = rows // n
         if not pieces:
             wpart[...] = wgrad.astype(BF16)
 
-        def span(ref, start, size):
-            return ref.at[pl.ds(pl.multiple_of(start, wrows), size)]
-
-        def piece(q):
-            return (lax.rem(q, 2) * half + q // 2) * wrows
-
-        swap = pltpu.make_async_remote_copy(
-            span(wpart, (1 - core) * half * wrows, half * wrows), wmate,
-            x_sem.at[0], x_sem.at[1], device_id={"dom": mate}, device_id_type=MESH,
-        )
-        swap.start()
-        swap.wait()
-        mine = wpart[pl.ds(pl.multiple_of(core * half * wrows, wrows), half * wrows), :]
-        wsend[...] = (mine.astype(F32) + wmate[...].astype(F32)).astype(BF16)
-        for q in line_peers:
-            dom_send(span(wsend, q // 2 * wrows, wrows), wrec.at[me // 2], ws_s, ws_r, q).start()
-        wrec[me // 2] = wsend[pl.ds(pl.multiple_of(me // 2 * wrows, wrows), wrows), :]
+        swap_start(1)
+        pair_sum(1)
     else:
         wg[...] = wgrad
         flush_wg = pltpu.make_async_copy(wg, wg_out, lsem.at[10])
@@ -308,14 +334,17 @@
             b_copy(h, q, True).start()
         gmrec[h][me] = msend[h, me]
         if scatter and h == 0:
-            for q in line_peers:
-                dom_recv(
-                    span(wsend, q // 2 * wrows, wrows), wrec.at[q // 2], ws_s, ws_r, q
-                ).wait_recv()
+            for g in used_groups:
+                for q in line_peers:
+                    line_copy(g, q, False).wait_recv()
             total = wrec[0].astype(F32)
             for p in range(1, half):
                 total = total + wrec[p].astype(F32)
-            wsum[...] = total.astype(BF16)
+            if pieces:
+                for k, source in enumerate((mf, near, far, across_both)):
+                    wsum[:, piece_rows(source)] = total[:, k * B : (k + 1) * B].astype(BF16)
+            else:
+                wsum[...] = total.astype(BF16)
             for q in line_peers:
                 dom_send(wsum, span(wg, piece(me), wrows), wg_s, wg_r, q).start()
             wg[pl.ds(pl.multiple_of(piece(me), wrows), wrows), :] = wsum[...]
@@ -359,7 +388,8 @@
             b_copy(h, q, True).wait_send()
     if scatter:
         for q in line_peers:
-            dom_send(span(wsend, q // 2 * wrows, wrows), wrec.at[me // 2], ws_s, ws_r, q).wait_send()
+            for g in used_groups:
+                line_copy(g, q, True).wait_send()
             dom_send(wsum, span(wg, piece(me), wrows), wg_s, wg_r, q).wait_send()
     flush_gn.wait()
     for copy in flush_gm:
@@ -451,9 +481,9 @@
             dma((n,)), dma((n,)),
             dma((2 * n,)), dma((2 * n,)),
             dma((2 * n,)), dma((2 * n,)),
+            dma((2 * n,)), dma((2 * n,)),
             dma((n,)), dma((n,)),
-            dma((n,)), dma((n,)),
-            dma((4,)),
+            dma((6,)),
         ],
         compiler_params=pltpu.CompilerParams(
             collective_id=0, has_side_effects=True, vmem_limit_bytes=62 * 1024 * 1024

time: 34.6 us -> 34.2 us (0.988)
  Pallas kernels: 33.1 us -> 32.7 us
    pallas_call x1, Pallas kernels: 31.3 us -> 30.9 us  [body(): pl.pallas_call(functools.partial(kernel, n, m, vb, scatter), out_shape=(j...]
where the time goes in v7:
time: 34.2 us; the launch traced here: 34 us
  Pallas kernels  32.7 us (96%)
  between operations  1.29 us (4%)
    pallas_call x1, Pallas kernels, body(): pl.pallas_call(functools.partial(kernel, n, m, vb, scatter), out_shape=(j...  30.9 us
    pallas_call x1, Pallas kernels, body(): pl.pallas_call(finish, out_shape=(jax.ShapeDtypeStruct(gn.shape, BF16), j...  1.84 us

profile of v7, /device:TPU:0, one launch (start us, length us, event | category | flops | bytes accessed | tf_op | source)
XLA Modules:
  0.0 34.0 jit_solution(8107766778555960261)
XLA Ops:
  1.3 30.9 %shard_map.112 = (bf16[128,768]{1,0:T(8,128)(2,1)}, bf16[128,1024]{1,0:T(8,128)(2,1)}, bf16[128,512]{1,0:T(8,128)(2,1)}) custom-call(s32[1,96]{1,0:T(1,128)} %bitcast.4, s32[1,96]{1,0:T(1,128)} %bitcast.5, s32[1,1]{1,0:T(1,128)} %bitcast.3.count_hbm, s32[1,8]{1,0:T(1,128)} %owner_hbm.1, s32[1,8]{1,0:T(1,128)} %local_hbm.1, bf16[128,768]{1,0:T(8,128)(2,1)} %g.1, ...), custom_call_target="tpu_custom_call" | custom-call | flops 402653184 | bytes 3932160 | tf_op jit(solution)/shard_map/pallas_call | solution.py:434
  32.2 1.8 %shard_map.113 = (bf16[128,768]{1,0:T(8,128)(2,1)}, bf16[128,1024]{1,0:T(8,128)(2,1)}, f32[128,512]{1,0:T(8,128)}) custom-call(bf16[128,768]{1,0:T(8,128)(2,1)} %get-tuple-element.6.gn, bf16[128,1024]{1,0:T(8,128)(2,1)} %get-tuple-element.7.gm, bf16[128,512]{1,0:T(8,128)(2,1)} %get-tuple-element.8.wg), custom_call_target="tpu_custom_call" | custom-call | tf_op jit(solution)/shard_map/pallas_call | solution.py:501

commit v8 on v7

--- a/solution.py
+++ b/solution.py
@@ -305,7 +305,7 @@
 
     for q in dom_peers:
         dom_recv(meta.at[q], mrec.at[q], m_s, m_r, q).wait_recv()
-    rc = min(32, half_rows)
+    rc = min(16, half_rows)
 
     def sum_rows(h, r, _):
         here = pl.ds(pl.multiple_of(r * rc, rc), rc)

time: 34.2 us -> 34.2 us (level)
  no operation moved by 1% of the time
where the time goes in v8:
time: 34.2 us; the launch traced here: 34 us
  Pallas kernels  32.7 us (96%)
  between operations  1.29 us (4%)
    pallas_call x1, Pallas kernels, body(): pl.pallas_call(functools.partial(kernel, n, m, vb, scatter), out_shape=(j...  30.9 us
    pallas_call x1, Pallas kernels, body(): pl.pallas_call(finish, out_shape=(jax.ShapeDtypeStruct(gn.shape, BF16), j...  1.84 us

profile of v8, /device:TPU:0, one launch (start us, length us, event | category | flops | bytes accessed | tf_op | source)
XLA Modules:
  0.0 34.0 jit_solution(18289485017810269720)
XLA Ops:
  1.3 30.9 %shard_map.112 = (bf16[128,768]{1,0:T(8,128)(2,1)}, bf16[128,1024]{1,0:T(8,128)(2,1)}, bf16[128,512]{1,0:T(8,128)(2,1)}) custom-call(s32[1,96]{1,0:T(1,128)} %bitcast.4, s32[1,96]{1,0:T(1,128)} %bitcast.5, s32[1,1]{1,0:T(1,128)} %bitcast.3.count_hbm, s32[1,8]{1,0:T(1,128)} %owner_hbm.1, s32[1,8]{1,0:T(1,128)} %local_hbm.1, bf16[128,768]{1,0:T(8,128)(2,1)} %g.1, ...), custom_call_target="tpu_custom_call" | custom-call | flops 402653184 | bytes 3932160 | tf_op jit(solution)/shard_map/pallas_call | solution.py:434
  32.2 1.8 %shard_map.113 = (bf16[128,768]{1,0:T(8,128)(2,1)}, bf16[128,1024]{1,0:T(8,128)(2,1)}, f32[128,512]{1,0:T(8,128)}) custom-call(bf16[128,768]{1,0:T(8,128)(2,1)} %get-tuple-element.6.gn, bf16[128,1024]{1,0:T(8,128)(2,1)} %get-tuple-element.7.gm, bf16[128,512]{1,0:T(8,128)(2,1)} %get-tuple-element.8.wg), custom_call_target="tpu_custom_call" | custom-call | tf_op jit(solution)/shard_map/pallas_call | solution.py:501
